TPU v7x, 128 devices: a whole 4x4x4 slice. The times are simulated.
128 devices in a mesh: seq: 32 (over y, x, core), exp: 4 (over z).
Axes of the slice: x: 4, y: 4, z: 4, core: 2. Of those that a mesh axis runs over, the one named last changes fastest.
Arguments:
- hidden: bfloat16 [256, 6144], P('seq', 'exp'), may hold values from -6 to 6
- queries: bfloat16 [256, 6144], P('seq', 'exp'), may hold values from -18 to 18
- suffix_row_keys: bfloat16 [256, 1024], P('seq', 'exp'), may hold values from -12 to 12
- suffix_row_values: bfloat16 [256, 1024], P('seq', 'exp'), may hold values from -6 to 6
- prefix_cached_keys: bfloat16 [65536, 1024], P('seq', 'exp'), may hold values from -10 to 10
- prefix_cached_values: bfloat16 [65536, 1024], P('seq', 'exp'), may hold values from -6 to 6
- expert_norm_gain: bfloat16 [6144], replicated, may hold values from 0.099609375 to 1.8984375
- router: bfloat16 [6144, 4], replicated, may hold values from -0.078125 to 0.078125
- gate_weight: bfloat16 [4, 6144, 8192], P('exp', None, 'seq'), may hold values from -0.078125 to 0.078125
- up_weight: bfloat16 [4, 6144, 8192], P('exp', None, 'seq'), may hold values from -0.078125 to 0.078125
- down_weight: bfloat16 [4, 8192, 6144], P('exp', 'seq'), may hold values from -0.0625 to 0.0625
- adapter_down_maps: bfloat16 [64, 4, 16, 8192], P(None, 'exp', None, 'seq'), may hold values from -0.0625 to 0.0625
- adapter_up_maps: bfloat16 [64, 4, 16, 6144], P('seq', 'exp'), may hold values from -1.5 to 1.5
- routes: int32 [256, 2], replicated, may hold values from 0 to 3, all different within a row; in each aligned block of 8 rows (0 to 7, 8 to 15, ...) at most 6 rows name the same one
- tenants: int32 [256], replicated, may hold values from 0 to 63, as said below
- lengths: int32 [64], replicated, may hold values from 1 to 7, as said below
Outputs:
- mixed: bfloat16 [256, 6144], P('seq', 'exp')
Inputs may be any that keep to these rules, and one draw needn't show every extreme that they name: `routes`: each row names two different experts; among the 8 rows of one index of seq no expert is named by more than 6 rows, a bound that some block reaches. `tenants`: row r belongs to tenant 2 * (r // 8) or the one after it; ids never fall along the rows; every tenant has at least one row. `lengths`: A tenant's length is at most its number of rows; some tenant has exactly 7 rows and that length.
All inputs are finite; a program needn't handle non-finite values.
Results may differ from a plain program's by a relative error of at most 0.017.
Values may be sent and summed in bfloat16 or wider, within the bound.
A program may use at most 192 MiB of HBM per device.

v0:
```python
import jax
import jax.numpy as jnp
from jax import lax
from jax.sharding import PartitionSpec as P

QUERY_HEADS = 48
KEY_VALUE_HEADS = 8
HEAD_SIZE = 128


NORM_EPS = 1e-05


def merged(x, axis, combine):
    everything = jax.tree.map(lambda part: lax.all_gather(part, axis), x)
    initial = jax.tree.map(lambda part: part[0], everything)

    def step(k, so_far):
        return combine(so_far, jax.tree.map(lambda part: part[k], everything))

    return lax.fori_loop(1, lax.axis_size(axis), step, initial)


def shard_partial(query_rows, key_rows, value_rows):
    row_count = query_rows.shape[0]
    block_rows = 512
    score_scale = HEAD_SIZE ** (-0.5)

    def one_block(query_block):
        scores = (
            lax.dot_general(
                query_block, key_rows, (((1,), (1,)), ((), ())), preferred_element_type=jnp.float32
            )
            * score_scale
        )
        row_peak = jnp.max(scores, axis=1)
        weights = jnp.exp(scores - row_peak[:, None])
        row_mass = jnp.sum(weights, axis=1)
        row_accum = jnp.dot(
            weights.astype(jnp.bfloat16), value_rows, preferred_element_type=jnp.float32
        )
        return (row_peak, row_mass, row_accum)

    peak_list, mass_list, accum_list = lax.map(
        one_block, query_rows.reshape(row_count // block_rows, block_rows, HEAD_SIZE)
    )
    return (
        peak_list.reshape(row_count),
        mass_list.reshape(row_count),
        accum_list.reshape(row_count, HEAD_SIZE),
    )


def combine_parts(earlier_part, later_part):
    overall = jnp.maximum(earlier_part[0], later_part[0])
    scale_early = jnp.exp(earlier_part[0] - overall)
    scale_late = jnp.exp(later_part[0] - overall)
    mass = earlier_part[1] * scale_early + later_part[1] * scale_late
    accum = earlier_part[2] * scale_early[..., None] + later_part[2] * scale_late[..., None]
    return (overall, mass, accum)


def on_device(
    hidden,
    queries,
    suffix_row_keys,
    suffix_row_values,
    prefix_cached_keys,
    prefix_cached_values,
    expert_norm_gain,
    router,
    gate_weight,
    up_weight,
    down_weight,
    adapter_down_maps,
    adapter_up_maps,
    routes,
    tenants,
    lengths,
):
    own_rows = hidden.shape[0]
    query_group_width = QUERY_HEADS // KEY_VALUE_HEADS
    kv_local = suffix_row_keys.shape[1] // HEAD_SIZE
    seq_count = lax.axis_size("seq")
    exp_count = lax.axis_size("exp")
    seq_index = lax.axis_index("seq")
    expert_index = lax.axis_index("exp")
    row_start = seq_index * own_rows
    score_scale = HEAD_SIZE ** (-0.5)
    all_queries = lax.all_gather(queries, "seq", axis=0, tiled=True)
    total_rows = all_queries.shape[0]
    peak_list, mass_list, accum_list = ([], [], [])
    for kv_head in range(kv_local):
        col_span = slice(
            kv_head * query_group_width * HEAD_SIZE, (kv_head + 1) * query_group_width * HEAD_SIZE
        )
        key_span = slice(kv_head * HEAD_SIZE, (kv_head + 1) * HEAD_SIZE)
        query_rows = all_queries[:, col_span].reshape(total_rows * query_group_width, HEAD_SIZE)
        row_peak, row_mass, row_accum = shard_partial(
            query_rows, prefix_cached_keys[:, key_span], prefix_cached_values[:, key_span]
        )
        peak_list.append(row_peak.reshape(total_rows, query_group_width))
        mass_list.append(row_mass.reshape(total_rows, query_group_width))
        accum_list.append(row_accum.reshape(total_rows, query_group_width, HEAD_SIZE))
    part_peak = jnp.concatenate(peak_list, axis=1)
    part_mass = jnp.concatenate(mass_list, axis=1)
    part_accum = jnp.concatenate(accum_list, axis=1)
    heads_local = part_peak.shape[1]
    merged_peak, merged_mass, merged_accum = merged(
        (part_peak, part_mass, part_accum), "seq", combine_parts
    )
    prefix_peak = lax.dynamic_slice_in_dim(merged_peak, row_start, own_rows, 0)
    prefix_mass = lax.dynamic_slice_in_dim(merged_mass, row_start, own_rows, 0)
    prefix_accum = lax.dynamic_slice_in_dim(merged_accum, row_start, own_rows, 0)
    own_tenants = lax.dynamic_slice_in_dim(tenants, row_start, own_rows, 0)
    row_ids = jnp.arange(own_rows)
    same_tenant = own_tenants[:, None] == own_tenants[None, :]
    before_row = row_ids[None, :] < row_ids[:, None]
    position = jnp.sum((same_tenant & before_row).astype(jnp.int32), axis=1)
    tenant_ids = jnp.arange(lengths.shape[0])
    row_length = jnp.sum(
        jnp.where(own_tenants[:, None] == tenant_ids[None, :], lengths[None, :], 0), axis=1
    )
    visible = (
        same_tenant
        & (position[None, :] <= position[:, None])
        & (position[None, :] < row_length[:, None])
    )
    visible_rep = jnp.repeat(visible, query_group_width, axis=0)
    suffix_peaks, suffix_masses, suffix_accums = ([], [], [])
    for kv_head in range(kv_local):
        col_span = slice(
            kv_head * query_group_width * HEAD_SIZE, (kv_head + 1) * query_group_width * HEAD_SIZE
        )
        key_span = slice(kv_head * HEAD_SIZE, (kv_head + 1) * HEAD_SIZE)
        query_rows = queries[:, col_span].reshape(own_rows * query_group_width, HEAD_SIZE)
        scores = (
            lax.dot_general(
                query_rows,
                suffix_row_keys[:, key_span],
                (((1,), (1,)), ((), ())),
                preferred_element_type=jnp.float32,
            )
            * score_scale
        )
        scores = jnp.where(visible_rep, scores, -1e30)
        row_peak = jnp.max(scores, axis=1)
        weights = jnp.where(visible_rep, jnp.exp(scores - row_peak[:, None]), 0.0)
        row_mass = jnp.sum(weights, axis=1)
        row_accum = jnp.dot(
            weights.astype(jnp.bfloat16),
            suffix_row_values[:, key_span],
            preferred_element_type=jnp.float32,
        )
        suffix_peaks.append(row_peak.reshape(own_rows, query_group_width))
        suffix_masses.append(row_mass.reshape(own_rows, query_group_width))
        suffix_accums.append(row_accum.reshape(own_rows, query_group_width, HEAD_SIZE))
    suffix_peak = jnp.concatenate(suffix_peaks, axis=1)
    suffix_mass = jnp.concatenate(suffix_masses, axis=1)
    suffix_accum = jnp.concatenate(suffix_accums, axis=1)
    overall, mass, accum = combine_parts(
        (prefix_peak, prefix_mass, prefix_accum), (suffix_peak, suffix_mass, suffix_accum)
    )
    prefix_attention = (accum / mass[..., None]).reshape(own_rows, heads_local * HEAD_SIZE)
    residual = (hidden.astype(jnp.float32) + prefix_attention).astype(jnp.bfloat16)
    gathered = lax.all_gather(residual[None], ("seq", "exp"), axis=0, tiled=True)
    gathered = (
        gathered.reshape(seq_count, exp_count, own_rows, residual.shape[1])
        .transpose(0, 2, 1, 3)
        .reshape(total_rows, -1)
    )
    resid_f = gathered.astype(jnp.float32)
    mean_square = jnp.mean(resid_f * resid_f, axis=1)
    normed = (
        resid_f
        * lax.rsqrt(mean_square + NORM_EPS)[:, None]
        * expert_norm_gain.astype(jnp.float32)[None, :]
    ).astype(jnp.bfloat16)
    width_full = normed.shape[1]
    routed_hit = (
        ((routes[:, 0] == expert_index) | (routes[:, 1] == expert_index))
        .astype(jnp.int32)
        .reshape(seq_count, own_rows)
    )
    slot_rank = jnp.cumsum(routed_hit, axis=1) - 1
    capacity = own_rows * 3 // 4
    slot_ids = jnp.arange(capacity)
    slot_match = (routed_hit[:, :, None] == 1) & (slot_rank[:, :, None] == slot_ids[None, None, :])
    local_row = jnp.sum(jnp.where(slot_match, row_ids[None, :, None], 0), axis=1)
    filled = jnp.any(slot_match, axis=1)
    global_row = (local_row + jnp.arange(seq_count)[:, None] * own_rows).reshape(-1)
    packed = jnp.take(normed, global_row, axis=0)
    gate_proj = jnp.dot(packed, gate_weight[0], preferred_element_type=jnp.float32)
    up_proj = jnp.dot(packed, up_weight[0], preferred_element_type=jnp.float32)
    hidden_activations = (jax.nn.silu(gate_proj) * up_proj).astype(jnp.bfloat16)
    down_proj = jnp.dot(hidden_activations, down_weight[0], preferred_element_type=jnp.float32)
    hidden_local = hidden_activations.shape[1]
    lowrank_gathered = lax.dot_general(
        hidden_activations,
        adapter_down_maps.reshape(-1, hidden_local),
        (((1,), (1,)), ((), ())),
        preferred_element_type=jnp.float32,
    )
    tenant_count = lengths.shape[0]
    packed_tenant = jnp.take(tenants, global_row, axis=0)
    tenant_pick = (packed_tenant[:, None] == tenant_ids[None, :]).astype(jnp.float32)
    low_rank = jnp.sum(
        lowrank_gathered.reshape(packed.shape[0], tenant_count, -1) * tenant_pick[:, :, None],
        axis=1,
    )
    rank_width = low_rank.shape[1]
    slot_valid = filled.reshape(-1).astype(jnp.float32)
    dense_down = (
        jnp.zeros((total_rows, width_full), jnp.float32)
        .at[global_row]
        .add(down_proj * slot_valid[:, None])
    )
    dense_low = (
        jnp.zeros((total_rows, rank_width), jnp.float32)
        .at[global_row]
        .add(low_rank * slot_valid[:, None])
    )
    own_down, own_low = (
        lax.psum_scatter(
            dense_down.astype(jnp.bfloat16), "seq", scatter_dimension=0, tiled=True
        ).astype(jnp.float32),
        lax.psum_scatter(
            dense_low.astype(jnp.bfloat16), "seq", scatter_dimension=0, tiled=True
        ).astype(jnp.float32),
    )
    tenants_here = adapter_up_maps.shape[0]
    tenant_local = own_tenants - tenants_here * seq_index
    local_hot = (tenant_local[:, None] == jnp.arange(tenants_here)[None, :]).astype(jnp.bfloat16)
    lowrank_padded = (local_hot[:, :, None] * own_low.astype(jnp.bfloat16)[:, None, :]).reshape(
        own_rows, -1
    )
    tenant_adapter = jnp.dot(
        lowrank_padded, adapter_up_maps.reshape(-1, width_full), preferred_element_type=jnp.float32
    )
    own_normed = lax.dynamic_slice_in_dim(normed, row_start, own_rows, 0)
    own_routes = lax.dynamic_slice_in_dim(routes, row_start, own_rows, 0)
    logits = jnp.dot(own_normed, router, preferred_element_type=jnp.float32)
    picked = jnp.take_along_axis(logits, own_routes, axis=1)
    share_first = jax.nn.sigmoid(picked[:, 0] - picked[:, 1])
    share_second = jax.nn.sigmoid(picked[:, 1] - picked[:, 0])
    route_weight = share_first * (own_routes[:, 0] == expert_index).astype(
        jnp.float32
    ) + share_second * (own_routes[:, 1] == expert_index).astype(jnp.float32)
    contrib = (own_down + tenant_adapter) * route_weight[:, None]
    summed = lax.psum_scatter(
        contrib.astype(jnp.bfloat16), "exp", scatter_dimension=1, tiled=True
    ).astype(jnp.float32)
    return (residual.astype(jnp.float32) + summed).astype(jnp.bfloat16)


def solution(mesh):
    in_specs = (
        P("seq", "exp"),
        P("seq", "exp"),
        P("seq", "exp"),
        P("seq", "exp"),
        P("seq", "exp"),
        P("seq", "exp"),
        P(),
        P(),
        P("exp", None, "seq"),
        P("exp", None, "seq"),
        P("exp", "seq", None),
        P(None, "exp", None, "seq"),
        P("seq", "exp", None, None),
        P(),
        P(),
        P(),
    )
    out_specs = P("seq", "exp")
    return jax.shard_map(
        on_device, mesh=mesh, in_specs=in_specs, out_specs=out_specs, check_vma=False
    )
```

profile of v0, /device:TPU:1, one launch (start us, length us, event | category | flops | bytes accessed | tf_op | source)
XLA Modules:
  0.0 748.6 jit_solution(4060110778831275486)
XLA Ops:
  6.5 26.8 %all_gather.24 = bf16[256,1536]{1,0:T(8,128)(2,1)S(1)} all-gather(bf16[8,1536]{1,0:T(8,128)(2,1)} %param.23), channel_id=1, replica_groups=mesh['seq'=32,'exp'=4] {'seq'}, dimensions={0}, use_global_device_ids=true | all-gather | bytes 811008 | tf_op jit(solution)/shard_map/all_gather | solution.py:90
  35.6 2.9 fusion.103
  40.0 16.9 %while.47 = (s32[]{:T(128)}, f32[3,512]{1,0:T(4,128)S(1)}, f32[3,512]{1,0:T(4,128)}, f32[3,512,128]{2,1,0:T(8,128)}, bf16[3,512,128]{2,1,0:T(8,128)(2,1)S(1)}, /...) while((s32[]{:T(128)}, f32[3,512]{1,0:T(4,128)S(1)}, ...), condition=%wide.region_3.4_spmd, body=%wide.region_0.3_spmd.sunk | while | flops 545258496 | bytes 16138885 | solution.py:44
  40.0 1.9 multiply_reduce_fusion.5
  45.7 1.9 multiply_reduce_fusion.5
  51.3 1.9 multiply_reduce_fusion.5
  57.0 2.2 reshape_reshape.30
  62.7 20.7 %while.48 = (s32[]{:T(128)}, f32[3,512]{1,0:T(4,128)}, f32[3,512]{1,0:T(4,128)}, f32[3,512,128]{2,1,0:T(8,128)}, bf16[3,512,128]{2,1,0:T(8,128)(2,1)S(1)}, /*ind...) while((s32[]{:T(128)}, f32[3,512]{1,0:T(4,128)}, f32[3,512]{1,0:T(4,128)}, ...), condition=%wide.region_7.8_spmd, body=%wide.region_4.7_spmd.sunk | while | flops 545258496 | bytes 16138885 | solution.py:44
  62.7 1.9 multiply_reduce_fusion.6
  69.6 1.9 multiply_reduce_fusion.6
  76.5 1.9 multiply_reduce_fusion.6
  83.4 2.3 reshape_reshape.31
  85.7 1.9 pad_maximum_fusion
  94.1 24.6 %all-gather.1 = f32[8192,12]{0,1:T(8,128)S(1)} all-gather(f32[256,12]{0,1:T(8,128)S(1)} %pad_maximum_fusion.2), channel_id=3, replica_groups=mesh['seq'=32,'exp'=4] {'seq'}, dimensions={0}, use_global_device_ids=true | all-gather | bytes 405504 | tf_op jit(solution)/shard_map/all_gather | solution.py:15
  120.2 22.6 %all-gather = f32[8192,12]{0,1:T(8,128)S(1)} all-gather(f32[256,12]{0,1:T(8,128)S(1)} %pad_maximum_fusion.1), channel_id=2, replica_groups=mesh['seq'=32,'exp'=4] {'seq'}, dimensions={0}, use_global_device_ids=true | all-gather | bytes 405504 | tf_op jit(solution)/shard_map/all_gather | solution.py:15
  144.2 1.8 slice_bitcast_fusion
  146.0 1.8 slice_bitcast_fusion.1
  147.8 100.5 %all-gather.7.cloned.1.call-done = f32[8192,12,128]{2,0,1:T(8,128)} async-done(((f32[256,12,128]{2,0,1:T(8,128)}), f32[8192,12,128]{2,0,1:T(8,128)}) %all-gather.7.cloned.1.call-update) | async-done | bytes 50331664 | tf_op jit(solution)/shard_map/all_gather | solution.py:15
  249.7 2.3 copy.81
  252.0 229.3 %while.49 = (s32[]{:T(128)}, f32[256,12]{0,1:T(8,128)S(1)}, f32[256,12]{0,1:T(8,128)S(1)}, f32[256,12,128]{2,1,0:T(8,128)}, f32[32,256,12]{1,0,2:T(8,128)}, /*in...) while((s32[]{:T(128)}, f32[256,12]{0,1:T(8,128)S(1)}, ...), condition=%wide.region_9.10_spmd, body=%wide.region_8.9_spmd.sunk | while | flops 1198085 | bytes 20668624 | solution.py:21
  255.3 2.8 fusion.142
  262.7 2.8 fusion.142
  270.1 2.8 fusion.142
  277.5 2.8 fusion.142
  282.8 1.7 constant_dynamic-slice_fusion.8
  284.9 2.8 fusion.142
  292.3 2.8 fusion.142
  299.7 2.8 fusion.142
  307.1 2.8 fusion.142
  314.5 2.8 fusion.142
  321.9 2.8 fusion.142
  329.3 2.8 fusion.142
  336.7 2.8 fusion.142
  344.1 2.8 fusion.142
  351.5 2.8 fusion.142
  358.8 2.8 fusion.142
  366.2 2.8 fusion.142
  373.6 2.8 fusion.142
  381.0 2.8 fusion.142
  388.4 2.8 fusion.142
  395.8 2.8 fusion.142
  403.2 2.8 fusion.142
  410.6 2.8 fusion.142
  418.0 2.8 fusion.142
  425.4 2.8 fusion.142
  432.8 2.8 fusion.142
  440.2 2.8 fusion.142
  447.6 2.8 fusion.142
  455.0 2.8 fusion.142
  462.4 2.8 fusion.142
  469.8 2.8 fusion.142
  477.2 2.8 fusion.142
  488.4 60.7 %all-gather.9.cloned.1.call-done = bf16[1024,1536]{1,0:T(8,128)(2,1)} async-done(((bf16[8,1536]{1,0:T(8,128)(2,1)}), bf16[1024,1536]{1,0:T(8,128)(2,1)}) %all-gather.9.cloned.1.call-update) | async-done | bytes 3145744 | tf_op jit(solution)/shard_map/all_gather | solution.py:166
  549.1 2.6 multiply_reduce_fusion.2
  552.0 2.7 convert_element_type.144
  554.7 2.6 multiply_convert_fusion
  557.3 7.9 %gather_fusion = bf16[192,6144]{1,0:T(8,128)(2,1)} fusion(bf16[256,6144]{1,0:T(8,128)(2,1)} %multiply_convert_fusion, s32[1024]{0:T(1024)S(1)} %pad_clamp_fusion), kind=kCustom, calls=%fused_computation | custom fusion | bytes 4719360 | tf_op jit(solution)/shard_map/jit(_take)/gather | solution.py:192
  565.3 3.6 fusion.46
  570.4 3.0 convolution_multiply_fusion
  573.4 11.1 %scatter_custom_fusion = f32[256,6144]{1,0:T(8,128)} fusion(s32[192]{0:T(256)S(1)} %bitcast.144, f32[192,6144]{1,0:T(8,128)} %convolution_multiply_fusion, f32[]{:T(128)} %constant.142.clone.1), kind=kCustom, calls=%fused_computation.58 | custom fusion | flops 1179648 | bytes 6291968 | tf_op jit(solution)/shard_map/scatter-add | solution.py:216
  584.5 4.9 convert_element_type.130
  595.3 121.4 %all-reduce = bf16[256,16]{1,0:T(8,128)(2,1)} all-reduce(bf16[256,16]{1,0:T(8,128)(2,1)} %convert_element_type.134), channel_id=7, replica_groups=mesh['seq'=32,'exp'=4] {'seq'}, use_global_device_ids=true, to_apply=%region_25.26.clone | all-reduce | flops 4096 | bytes 16384
  720.2 1.7 fusion.42
  721.9 18.8 %reduce-scatter.5.cloned.1.call-done = bf16[8,1536]{1,0:T(8,128)(2,1)} async-done(((bf16[8,6144]{1,0:T(8,128)(2,1)}), bf16[8,1536]{1,0:T(8,128)(2,1)}) %reduce-scatter.5.cloned.1.call-update) | async-done | bytes 24592 | tf_op jit(solution)/shard_map/reduce_scatter | solution.py:250
  (459 shorter events, 203.2 us)
Async XLA Ops:
  6.5 563.8 %copy-start = (bf16[1,256,6144]{2,1,0:T(8,128)(2,1)S(1)}, bf16[1,256,6144]{2,1,0:T(8,128)(2,1)}, u32[]{:S(2)}) copy-start(bf16[1,256,6144]{2,1,0:T(8,128)(2,1)} %param.32) | copy-start | bytes 9437188
  6.5 241.8 %all-gather.7.cloned.1.call-start = ((), (), s32[]{:S(2)}) async-start(), calls=%async_computation.4 | async-start | bytes 51904512 | tf_op jit(solution)/shard_map/all_gather | solution.py:15
  40.0 1.9 copy-start.5
  45.7 1.9 copy-start.5
  51.3 1.9 copy-start.5
  62.7 1.9 copy-start.4
  69.6 1.9 copy-start.4
  76.5 1.9 copy-start.4
  87.5 1.8 copy-start.1
  87.6 2.5 copy-start.19
  87.6 3.0 copy-start.8
  87.6 3.0 copy-start.15
  87.6 6.1 copy-start.9
  87.6 6.3 copy-start.11
  87.6 32.3 %copy-start.10 = (f32[3,512]{1,0:T(4,128)S(1)}, f32[3,512]{1,0:T(4,128)}, u32[]{:S(2)}) copy-start(f32[3,512]{1,0:T(4,128)} %get-tuple-element.262) | copy-start | bytes 18436
  89.2 54.5 %copy-start.16 = (bf16[8,256]{1,0:T(8,128)(2,1)S(1)}, bf16[8,256]{1,0:T(8,128)(2,1)}, u32[]{:S(2)}) copy-start(bf16[8,256]{1,0:T(8,128)(2,1)} %param.25) | copy-start | bytes 12292
  89.3 459.8 %all-gather.9.cloned.1.call-start = ((), (), s32[]{:S(2)}) async-start(), calls=%async_computation.5 | async-start | bytes 3170304 | tf_op jit(solution)/shard_map/all_gather | solution.py:166
  248.3 1.4 slice-start
  252.0 229.6 %copy-start.13 = (f32[8,6]{1,0:T(8,128)S(1)}, f32[8,6]{1,0:T(8,128)}, u32[]{:S(2)}) copy-start(f32[8,6]{1,0:T(8,128)} %reshape.253) | copy-start | bytes 580
  252.0 231.3 %copy-start.12 = (bf16[8,1536]{1,0:T(8,128)(2,1)S(1)}, bf16[8,1536]{1,0:T(8,128)(2,1)}, u32[]{:S(2)}) copy-start(bf16[8,1536]{1,0:T(8,128)(2,1)} %param.22) | copy-start | bytes 73732
  253.2 2.1 copy-start.2
  258.1 1.3 copy-start.3
  260.6 2.1 copy-start.2
  268.0 2.1 copy-start.2
  275.4 2.1 copy-start.2
  282.8 2.1 copy-start.2
  287.7 1.3 copy-start.3
  290.2 2.1 copy-start.2
  295.1 1.3 copy-start.3
  297.6 2.1 copy-start.2
  302.5 1.3 copy-start.3
  305.0 2.1 copy-start.2
  309.9 1.3 copy-start.3
  312.4 2.1 copy-start.2
  317.3 1.3 copy-start.3
  319.8 2.1 copy-start.2
  324.7 1.3 copy-start.3
  327.2 2.1 copy-start.2
  334.6 2.1 copy-start.2
  342.0 2.1 copy-start.2
  349.4 2.1 copy-start.2
  356.8 2.1 copy-start.2
  364.2 2.1 copy-start.2
  371.6 2.1 copy-start.2
  379.0 2.1 copy-start.2
  386.4 2.1 copy-start.2
  393.8 2.1 copy-start.2
  401.2 2.1 copy-start.2
  408.6 2.1 copy-start.2
  416.0 2.1 copy-start.2
  423.4 2.1 copy-start.2
  430.8 2.1 copy-start.2
  438.1 2.1 copy-start.2
  445.5 2.1 copy-start.2
  452.9 2.1 copy-start.2
  460.3 2.1 copy-start.2
  467.7 2.1 copy-start.2
  475.1 2.1 copy-start.2
  484.0 236.2 %reduce-scatter.3.cloned.1.call-start = ((), (), s32[]{:S(2)}) async-start(), calls=%async_computation.2 | async-start | bytes 3244032 | tf_op jit(solution)/shard_map/reduce_scatter | solution.py:224
  565.3 3.6 copy-start.6
  565.3 4.2 copy-start.18
  589.4 2.3 copy-start.17
  589.4 151.3 %reduce-scatter.5.cloned.1.call-start = ((), (), s32[]{:S(2)}) async-start(), calls=%async_computation.3 | async-start | bytes 122880 | tf_op jit(solution)/shard_map/reduce_scatter | solution.py:250
  595.3 124.9 %copy-start.7 = (bf16[2,1,16,6144]{3,2,1,0:T(8,128)(2,1)S(1)}, bf16[2,1,16,6144]{3,2,1,0:T(8,128)(2,1)}, u32[]{:S(2)}) copy-start(bf16[2,1,16,6144]{3,2,1,0:T(8,128)(2,1)} %param.34) | copy-start | bytes 1179652
  (26 other events, 33.2 us)
Sparse Core Ops, SparseCore 0:
  89.4 158.8 all-gather.6
  484.1 64.9 all-gather.8
  589.6 75.5 reduce-scatter.2
  722.0 18.6 reduce-scatter.4
where the time goes:
time: 753 us; the launch traced here: 749 us
  local copies, waits for them, and re-layouts  198 us (26%)
  blocking collectives  195 us (26%)
  waiting for transfers between devices  180 us (24%)
  other arithmetic  127 us (17%)
  matrix products  32.9 us (4%)
  between operations  14.1 us (2%)
    unnamed x1, blocking collectives  121 us
    all_gather x1, waiting for transfers between devices, merged(): everything = jax.tree.map(lambda part: lax.all_gather(part, axis), x)  101 us
    add x31, other arithmetic, combine_parts(): earlier_part[2] * scale_early[..., None]  86.5 us
    dynamic_slice x62, local copies, waits for them, and re-layouts, step(): return combine(so_far, jax.tree.map(lambda part: part[k], everything))  81.5 us
    all_gather x1, waiting for transfers between devices, on_device(): lax.all_gather(residual[None], ('seq', 'exp'), axis=0, tiled=True)  60.7 us
    while x136, local copies, waits for them, and re-layouts  52.3 us
    all_gather x2, blocking collectives, merged(): everything = jax.tree.map(lambda part: lax.all_gather(part, axis), x)  47.2 us
    all_gather x1, blocking collectives, on_device(): all_queries = lax.all_gather(queries, 'seq', axis=0, tiled=True)  26.8 us
  transfers between devices with their start and end apart: 4, of which 3 were waited for; matrix products, arithmetic and copies ran while one was open for 3% of the time, Pallas kernels for 0%

commit v1 on v0

v1 whole, which is shorter than its diff:
```python
import functools

import jax
import jax.numpy as jnp
from jax import lax
from jax.experimental import pallas as pl
from jax.experimental.pallas import tpu as pltpu
from jax.sharding import PartitionSpec as P

MESH = pl.DeviceIdType.MESH
F32 = jnp.float32
BF16 = jnp.bfloat16

HEAD = 128
GROUP = 6
KV = 2
HEADS = KV * GROUP
ROWS = 8
SEQ = 32
EXP = 4
CHIPS = SEQ // 2
PAIR = 2 * ROWS
TOTAL = SEQ * ROWS
WIDTH = 6144
HALF = WIDTH // 2
QUARTER = WIDTH // EXP
PREFIX = 2048
UNITS = 256
QB = GROUP * ROWS
BLK = KV * QB
MSG = BLK + 16
EXT = HALF + 128
CUT = 1536
NORM_EPS = 1e-05
LOG2E = 1.4426950408889634
SCALE2 = HEAD**-0.5 * LOG2E


def dot(a, b):
    return jnp.dot(a, b, preferred_element_type=F32)


def dot_t(a, b):
    return lax.dot_general(a, b, (((1,), (1,)), ((), ())), preferred_element_type=F32)


def iota(shape, dim):
    return lax.broadcasted_iota(jnp.int32, shape, dim)


def three_parts(v):
    high = v.astype(BF16).astype(F32)
    rest = v - high
    mid = rest.astype(BF16).astype(F32)
    low = rest - mid
    ax = v.ndim - 1
    return high + pltpu.roll(mid, 16, ax) + pltpu.roll(low, 32, ax)


def whole_of(p):
    ax = p.ndim - 1
    return p + pltpu.roll(p, 128 - 16, ax) + pltpu.roll(p, 128 - 32, ax)


def kernel(
    hid, qry, skey, sval, pk, pv, gain, rout, wg, wu, wd, adn, aup, routes, tenants, lengths,
    out,
    qall, kbuf, vext, sbuf, pbuf, suf_o, suf_l, rsnd, rbuf, xbuf, wgb, wub, wdb, adnb, upb,
    accg, accu, s1snd, s1rcv, own, p2, r2a, r2b, p3a, p3b, r3a, r3b, fsnd, fbuf, resid_ref,
    lsem, qs, qf, qr, ps, pr, rs, rr, xs, xf, xr, ups, upr, s1s, s1r, as2, ar2, bs2, br2,
    as3, ar3, bs3, br3, fs, fr,
):
    s = lax.axis_index("seq")
    z = lax.axis_index("exp")
    k = lax.rem(s, 2)
    c = lax.div(s, 2)
    x = lax.rem(c, 4)
    y = lax.div(c, 4)
    sib = s + 1 - 2 * k

    def remote(src, dst, ssem, rsem, seq, exp):
        return pltpu.make_async_remote_copy(
            src_ref=src, dst_ref=dst, send_sem=ssem, recv_sem=rsem,
            device_id=(seq, exp), device_id_type=MESH,
        )

    def each(n, body, first=0):
        def step(i, carry):
            body(i)
            return carry

        lax.fori_loop(first, n, step, 0)

    k_half = pl.multiple_of(k * HALF, HALF)
    up_row = pl.multiple_of(64 * lax.rem(c, 2) + 32 * k, 32)
    loads = [
        (pk, kbuf),
        (pv.at[:, pl.ds(0, HEAD)], vext.at[0, :, pl.ds(0, HEAD)]),
        (pv.at[:, pl.ds(HEAD, HEAD)], vext.at[1, :, pl.ds(0, HEAD)]),
        (wg, wgb),
        (wu, wub),
        (wd, wdb),
        (adn, adnb),
        (aup.at[:, pl.ds(k_half, HALF)], upb.at[pl.ds(up_row, 32), :]),
    ]
    loads = [pltpu.make_async_copy(a, b, lsem.at[i]) for i, (a, b) in enumerate(loads)]
    for cp in loads:
        cp.start()

    q = qry[...].astype(F32)
    for g in range(KV):
        heads = [q[:, (g * GROUP + j) * HEAD : (g * GROUP + j + 1) * HEAD] for j in range(GROUP)]
        qall[g, s] = jnp.concatenate(heads, axis=0).astype(BF16)

    barrier = pltpu.get_barrier_semaphore()

    def greet_plane(i):
        pl.semaphore_signal(barrier, inc=1, device_id=(lax.rem(s + i, SEQ), z), device_id_type=MESH)

    each(SEQ, greet_plane, 1)
    for d in range(1, EXP):
        for other in (s, sib):
            pl.semaphore_signal(
                barrier, inc=1, device_id=(other, lax.rem(z + d, EXP)), device_id_type=MESH
            )
    vext[:, :, HEAD:] = jnp.ones((KV, PREFIX, HEAD), BF16)
    other_rows = pl.multiple_of(64 - 64 * lax.rem(c, 2), 64)
    upb[pl.ds(other_rows, 64), :] = jnp.zeros((64, HALF), BF16)
    pl.semaphore_wait(barrier, SEQ - 1 + 2 * (EXP - 1))

    def chip_at(i):
        return lax.rem(y + 4 - i // 4, 4) * 4 + lax.rem(x + i % 4, 4)

    def q_copy(block, to, ssem):
        return remote(qall.at[:, block], qall.at[:, block], ssem, qr.at[block], to, z)

    def q_send(i):
        return q_copy(s, chip_at(i) * 2 + k, qs.at[i])

    def q_sib():
        return q_copy(s, sib, qs.at[0])

    q_sib().start()
    each(CHIPS, lambda i: q_send(i).start(), 1)
    up_other = pl.multiple_of(HALF - k * HALF, HALF)

    def up_copy():
        return remote(
            aup.at[:, pl.ds(up_other, HALF)], upb.at[pl.ds(up_row, 32), :], ups.at[0], upr.at[0], sib, z
        )

    up_copy().start()

    row8 = iota((ROWS, 128), 0)
    lane8 = iota((ROWS, 128), 1)
    ten = [tenants[s * ROWS + i] for i in range(ROWS)]
    pos = []
    for i in range(ROWS):
        p = jnp.int32(0)
        for j in range(i):
            p = p + (ten[i] == ten[j]).astype(jnp.int32)
        pos.append(p)
    lens = [lengths[ten[i]] for i in range(ROWS)]

    def spread(values, at):
        got = jnp.full((ROWS, 128), -1, jnp.int32)
        for i, v in enumerate(values):
            got = jnp.where(at == i, v, got)
        return got

    ten_r, ten_c = spread(ten, row8), spread(ten, lane8)
    pos_r, pos_c = spread(pos, row8), spread(pos, lane8)
    len_r = spread(lens, row8)
    visible = (lane8 < ROWS) & (ten_r == ten_c) & (pos_c <= pos_r) & (pos_c < len_r)
    visible = jnp.broadcast_to(visible[None], (GROUP, ROWS, 128))
    sk = skey[...].astype(F32)
    sv = sval[...].astype(F32)
    fill = jnp.zeros((128 - ROWS, HEAD), F32)
    stat = jnp.zeros((ROWS, 128), F32)
    for g in range(KV):
        kg = jnp.concatenate([sk[:, g * HEAD : (g + 1) * HEAD], fill], axis=0).astype(BF16)
        vg = jnp.concatenate([sv[:, g * HEAD : (g + 1) * HEAD], fill], axis=0).astype(BF16)
        sc = dot_t(qall[g, s], kg).reshape(GROUP, ROWS, 128)
        sc = jnp.where(visible, sc, -1e30)
        m = jnp.max(sc, axis=2, keepdims=True)
        w = jnp.where(visible, jnp.exp2((sc - m) * SCALE2), 0.0)
        mass = jnp.sum(w, axis=2, keepdims=True)
        acc = dot(w.reshape(QB, 128).astype(BF16), vg).reshape(GROUP, ROWS, HEAD)
        suf_o[g * GROUP : (g + 1) * GROUP] = acc / mass
        lse = jnp.broadcast_to(m * SCALE2 + jnp.log2(mass), (GROUP, ROWS, 128))
        for j in range(GROUP):
            stat = jnp.where(lane8 == g * GROUP + j, lse[j], stat)
    suf_l[...] = stat

    for cp in loads[:3]:
        cp.wait()

    def q_forward(yy):
        def one(i):
            chip = yy * 4 + lax.rem(x + i, 4)

            @pl.when(chip != c)
            def _():
                block = chip * 2 + k
                q_copy(block, sib, qf.at[chip]).wait_recv()
                q_copy(block, sib, qf.at[chip]).start()

        each(4, one)

    def p_copy(block, to):
        return remote(sbuf.at[block], pbuf.at[s], ps.at[block], pr.at[s], to, z)

    def attend(dy):
        yy = lax.rem(y + dy, 4)

        @pl.when(dy == 0)
        def _():
            q_forward(y)

        @pl.when(dy == 1)
        def _():
            for d in range(1, 4):
                q_forward(lax.rem(y + d, 4))

        def from_sib(i):
            block = (yy * 4 + i) * 2 + 1 - k
            q_copy(block, sib, qf.at[0]).wait_recv()

        each(4, from_sib)
        lane = iota((8, ROWS, 128), 2)
        stat = jnp.zeros((8, ROWS, 128), F32)
        for g in range(KV):
            qg = qall[g, pl.ds(yy * 8, 8)].reshape(8 * QB, HEAD)
            sc = dot_t(qg, kbuf[:, g * HEAD : (g + 1) * HEAD])
            m = jnp.max(sc, axis=1, keepdims=True) * SCALE2
            w = jnp.exp2(sc * SCALE2 - m).astype(BF16)
            acc = dot(w, vext[g])
            mass = acc[:, HEAD:]
            o = acc[:, :HEAD] / mass
            sbuf[pl.ds(yy * 8, 8), g * QB : (g + 1) * QB, :] = o.astype(BF16).reshape(8, QB, HEAD)
            lse = (m + jnp.log2(mass)).reshape(8, GROUP, ROWS, 128)
            for j in range(GROUP):
                stat = jnp.where(lane == g * GROUP + j, lse[:, j], stat)
        parts = three_parts(stat)
        parts = jnp.concatenate([parts, jnp.zeros_like(parts)], axis=1).astype(BF16)
        sbuf[pl.ds(yy * 8, 8), BLK:, :] = parts

        def p_send(i):
            block = yy * 8 + lax.rem(lax.rem(s, 8) + i, 8)

            @pl.when(block != s)
            def _():
                p_copy(block, block).start()

        each(8, p_send)

    each(4, attend)
    keep = pltpu.make_async_copy(sbuf.at[s], pbuf.at[s], lsem.at[8])
    keep.start()
    keep.wait()

    def p_wait(i):
        @pl.when(i != s)
        def _():
            remote(sbuf.at[i], pbuf.at[i], ps.at[i], pr.at[i], i, z).wait_recv()

    each(SEQ, p_wait)
    lses = whole_of(pbuf[:, BLK:, :].astype(F32)[:, :ROWS])
    top = jnp.maximum(jnp.max(lses, axis=0), suf_l[...])
    shares = jnp.exp2(lses - top[None])
    suf_share = jnp.exp2(suf_l[...] - top)
    inverse = 1.0 / (jnp.sum(shares, axis=0) + suf_share)
    suf_share = suf_share * inverse
    att = [suf_share[:, h : h + 1] * suf_o[h] for h in range(HEADS)]
    for i in range(SEQ):
        part = pbuf[i, 0:BLK, :].astype(F32)
        share = shares[i] * inverse
        for h in range(HEADS):
            att[h] = att[h] + share[:, h : h + 1] * part[h * ROWS : (h + 1) * ROWS]
    resid = hid[...].astype(F32) + jnp.concatenate(att, axis=1)
    resid = resid.astype(BF16).astype(F32)
    resid_ref[...] = resid
    cols = QUARTER // 2
    rsnd[...] = jnp.concatenate([resid[:, :cols], resid[:, cols:]], axis=0).astype(BF16)

    to_core = lax.div(z, 2)
    r_slot = k * 2 + lax.rem(z, 2)

    def r_copy(d):
        return remote(
            rsnd, rbuf.at[r_slot], rs.at[d], rr.at[r_slot], c * 2 + to_core, lax.rem(z + d, EXP)
        )

    for d in range(1, EXP):
        r_copy(d).start()

    @pl.when(to_core != k)
    def _():
        r_copy(0).start()

    @pl.when(to_core == k)
    def _():
        rbuf[r_slot] = rsnd[...]

    for kk in range(2):
        for j in range(2):

            @pl.when(~((kk == k) & (2 * k + j == z)))
            def _():
                slot = kk * 2 + j
                remote(
                    rsnd, rbuf.at[slot], rs.at[0], rr.at[slot], c * 2 + kk, 2 * k + j
                ).wait_recv()

    halves = []
    for kk in range(2):
        got = [rbuf[kk * 2 + j].astype(F32) for j in range(2)]
        halves.append(
            jnp.concatenate([got[0][:ROWS], got[0][ROWS:], got[1][:ROWS], got[1][ROWS:]], axis=1)
        )
    both = jnp.concatenate(halves, axis=0)
    squares = jnp.sum(both * both, axis=1, keepdims=True)
    gains = gain[...].astype(F32)
    gains = jnp.where(k == 0, gains[:, :HALF], gains[:, HALF:])
    own_rows = pl.multiple_of(c * PAIR, PAIR)
    xbuf[k, pl.ds(own_rows, PAIR), 0:HALF] = (both * gains).astype(BF16)
    squares = jnp.where(iota((PAIR, 128), 1) == 0, squares, 0.0)
    xbuf[k, pl.ds(own_rows, PAIR), HALF:] = three_parts(squares).astype(BF16)

    def x_copy(half, chip, to, ssem):
        at = pl.ds(pl.multiple_of(chip * PAIR, PAIR), PAIR)
        return remote(xbuf.at[half, at, :], xbuf.at[half, at, :], ssem, xr.at[half, chip], to, z)

    x_copy(k, c, sib, xs.at[0]).start()
    each(CHIPS, lambda i: x_copy(k, c, chip_at(i) * 2 + k, xs.at[i]).start(), 1)

    def x_forward(i):
        chip = lax.rem(y + i // 4, 4) * 4 + lax.rem(x + i % 4, 4)
        x_copy(k, chip, sib, xf.at[chip]).wait_recv()
        x_copy(k, chip, sib, xf.at[chip]).start()

    each(CHIPS, x_forward, 1)

    for cp in loads[3:5]:
        cp.wait()
    step_cols = 1024

    def project(half, first):
        def one(i):
            at = pl.multiple_of(i * step_cols, step_cols)
            rows = pl.ds(pl.multiple_of(half * HALF + at, step_cols), step_cols)
            xs_ = xbuf[half, :, pl.ds(at, step_cols)]
            g_ = dot(xs_, wgb[rows, :])
            u_ = dot(xs_, wub[rows, :])
            accg[...] = accg[...] + g_
            accu[...] = accu[...] + u_

        if first:
            accg[...] = jnp.zeros_like(accg)
            accu[...] = jnp.zeros_like(accu)
        each(HALF // step_cols, one)

    project(k, True)
    each(CHIPS, lambda i: x_copy(1 - k, i, sib, xf.at[0]).wait_recv())
    project(1 - k, False)

    def inverse_norm(parts):
        total = jnp.sum(parts, axis=1, keepdims=True)
        return lax.rsqrt(total / WIDTH + NORM_EPS)

    scale = inverse_norm(xbuf[0, :, HALF:].astype(F32) + xbuf[1, :, HALF:].astype(F32))
    gate = accg[...] * scale
    units = (gate / (1.0 + jnp.exp(-gate)) * (accu[...] * scale)).astype(BF16)

    for cp in loads[5:]:
        cp.wait()
    low = [
        dot_t(units[i * 32 : (i + 1) * 32], adnb[i * 128 : (i + 1) * 128, :])
        for i in range(CHIPS // 2)
    ]
    low = jnp.concatenate(low, axis=0)
    s1snd[:, HALF:] = low.astype(BF16)
    own[:, HALF:] = low

    part = 768
    n_parts = HALF // part
    widths = [part] * (n_parts - 1) + [part + 128]

    def s1_copy(i):
        at = pl.ds(i * part, widths[i])
        return remote(s1snd.at[:, at], s1rcv.at[:, at], s1s.at[i], s1r.at[i], sib, z)

    def down(half, i):
        at = pl.multiple_of(half * HALF + i * part, 128)
        return dot(units, wdb[:, pl.ds(at, part)])

    for i in range(n_parts):
        s1snd[:, i * part : (i + 1) * part] = down(1 - k, i).astype(BF16)
        s1_copy(i).start()
    for i in range(n_parts):
        own[:, i * part : (i + 1) * part] = down(k, i)

    def a2_copy(d):
        xx = lax.rem(x + d, 4)
        return remote(
            p2.at[:, xx, :, pl.ds(0, CUT)], r2a.at[x], as2.at[d], ar2.at[x], (y * 4 + xx) * 2 + k, z
        )

    def b2_copy(d):
        yy = lax.rem(y + d, 4)
        return remote(
            p2.at[yy, :, :, pl.ds(CUT, EXT - CUT)], r2b.at[y], bs2.at[d], br2.at[y],
            (yy * 4 + x) * 2 + k, z,
        )

    for i in range(n_parts):
        s1_copy(i).wait_recv()
        at = slice(i * part, i * part + widths[i])
        both = own[:, at] + s1rcv[:, at].astype(F32)
        p2[:, :, :, at] = both.astype(BF16).reshape(4, 4, PAIR, widths[i])
        if (i + 1) * part == CUT:
            for d in (2, 1, 3):
                a2_copy(d).start()
    for d in (2, 1, 3):
        b2_copy(d).start()

    row16 = iota((PAIR, 128), 0)

    def column(load):
        got = jnp.zeros((PAIR, 128), jnp.int32)
        for i in range(PAIR):
            got = jnp.where(row16 == i, load(c * PAIR + i), got)
        return got

    first = column(lambda i: routes[0, i])
    second = column(lambda i: routes[1, i])
    ten_rows = column(lambda i: tenants[i])
    xa = xbuf[0, pl.ds(own_rows, PAIR), :].astype(F32)
    xb = xbuf[1, pl.ds(own_rows, PAIR), :].astype(F32)
    own_scale = inverse_norm(xa[:, HALF:] + xb[:, HALF:])
    rt = rout[...].astype(F32)
    other = first + second - z
    mine = jnp.zeros((PAIR, 128), F32)
    theirs = jnp.zeros((PAIR, 128), F32)
    for e in range(EXP):
        logit = jnp.sum(xa[:, :HALF] * rt[e : e + 1, :HALF], axis=1, keepdims=True)
        logit = logit + jnp.sum(xb[:, :HALF] * rt[e : e + 1, HALF:], axis=1, keepdims=True)
        logit = logit * own_scale
        mine = jnp.where(z == e, logit, mine)
        theirs = jnp.where(other == e, logit, theirs)
    share = 1.0 / (1.0 + jnp.exp(theirs - mine))
    share = jnp.where((first == z) | (second == z), share, 0.0)[:, 0:1]

    def a2_wait(d):
        xx = lax.rem(x + d, 4)
        remote(
            p2.at[:, x, :, pl.ds(0, CUT)], r2a.at[xx], as2.at[0], ar2.at[xx],
            (y * 4 + xx) * 2 + k, z,
        ).wait_recv()
        return xx

    def b2_wait(d):
        yy = lax.rem(y + d, 4)
        remote(
            p2.at[y, :, :, pl.ds(CUT, EXT - CUT)], r2b.at[yy], bs2.at[0], br2.at[yy],
            (yy * 4 + x) * 2 + k, z,
        ).wait_recv()
        return yy

    total = p2[:, x, :, 0:CUT].astype(F32)
    for d in (1, 3, 2):
        total = total + r2a[a2_wait(d)].astype(F32)
    p3a[...] = total.astype(BF16)

    def a3_copy(d):
        yy = lax.rem(y + d, 4)
        return remote(p3a.at[yy], r3a.at[y], as3.at[d], ar3.at[y], (yy * 4 + x) * 2 + k, z)

    for d in (2, 1, 3):
        a3_copy(d).start()
    total = p2[y, :, :, CUT:].astype(F32)
    for d in (1, 3, 2):
        total = total + r2b[b2_wait(d)].astype(F32)
    p3b[...] = total.astype(BF16)

    def b3_copy(d):
        xx = lax.rem(x + d, 4)
        return remote(p3b.at[xx], r3b.at[x], bs3.at[d], br3.at[x], (y * 4 + xx) * 2 + k, z)

    for d in (2, 1, 3):
        b3_copy(d).start()

    sum_a = p3a[y].astype(F32)
    for d in (1, 3, 2):
        yy = lax.rem(y + d, 4)
        remote(p3a.at[y], r3a.at[yy], as3.at[0], ar3.at[yy], (yy * 4 + x) * 2 + k, z).wait_recv()
        sum_a = sum_a + r3a[yy].astype(F32)
    sum_b = p3b[x].astype(F32)
    for d in (1, 3, 2):
        xx = lax.rem(x + d, 4)
        remote(p3b.at[x], r3b.at[xx], bs3.at[0], br3.at[xx], (y * 4 + xx) * 2 + k, z).wait_recv()
        sum_b = sum_b + r3b[xx].astype(F32)

    up_copy().wait_recv()
    low = sum_b[:, HALF - CUT :]
    low = jnp.where(lax.div(iota((PAIR, 128), 1), 16) == lax.rem(ten_rows, 8), low, 0.0)
    adapter = dot(low.astype(BF16), upb[...])
    contrib = (jnp.concatenate([sum_a, sum_b[:, : HALF - CUT]], axis=1) + adapter) * share

    def f_copy(kk, j):
        slot = kk * 2 + j
        return remote(fsnd.at[slot], fbuf.at[z], fs.at[slot], fr.at[z], c * 2 + kk, 2 * k + j)

    for kk in range(2):
        for j in range(2):
            slot = kk * 2 + j
            rows = contrib[kk * ROWS : (kk + 1) * ROWS, j * QUARTER : (j + 1) * QUARTER]
            fsnd[slot] = jnp.concatenate([rows[:, :cols], rows[:, cols:]], axis=0).astype(BF16)
            is_self = (kk == k) & (2 * k + j == z)

            @pl.when(~is_self)
            def _():
                f_copy(kk, j).start()

            @pl.when(is_self)
            def _():
                fbuf[z] = fsnd[slot]

    for e in range(EXP):

        @pl.when(~((to_core == k) & (e == z)))
        def _():
            remote(fsnd.at[0], fbuf.at[e], fs.at[0], fr.at[e], c * 2 + to_core, e).wait_recv()

    got = fbuf[...].astype(F32)
    got = got[0] + got[1] + got[2] + got[3]
    got = jnp.concatenate([got[:ROWS], got[ROWS:]], axis=1)
    out[...] = (resid_ref[...] + got).astype(BF16)

    q_sib().wait_send()
    each(CHIPS, lambda i: q_send(i).wait_send(), 1)
    up_copy().wait_send()

    def sends_of_chip(i):
        @pl.when(i != c)
        def _():
            q_copy(i * 2 + k, sib, qf.at[i]).wait_send()
            x_copy(k, i, sib, xf.at[i]).wait_send()

    each(CHIPS, sends_of_chip)

    def sends_of_block(i):
        @pl.when(i != s)
        def _():
            p_copy(i, i).wait_send()

    each(SEQ, sends_of_block)
    for d in range(1, EXP):
        r_copy(d).wait_send()

    @pl.when(to_core != k)
    def _():
        r_copy(0).wait_send()

    x_copy(k, c, sib, xs.at[0]).wait_send()
    each(CHIPS, lambda i: x_copy(k, c, chip_at(i) * 2 + k, xs.at[i]).wait_send(), 1)
    for i in range(n_parts):
        s1_copy(i).wait_send()
    for d in (2, 1, 3):
        a2_copy(d).wait_send()
        b2_copy(d).wait_send()
        a3_copy(d).wait_send()
        b3_copy(d).wait_send()
    for kk in range(2):
        for j in range(2):

            @pl.when(~((kk == k) & (2 * k + j == z)))
            def _():
                f_copy(kk, j).wait_send()


def on_device(
    hidden, queries, suffix_row_keys, suffix_row_values, prefix_cached_keys, prefix_cached_values,
    expert_norm_gain, router, gate_weight, up_weight, down_weight, adapter_down_maps,
    adapter_up_maps, routes, tenants, lengths,
):
    vmem = pl.BlockSpec(memory_space=pltpu.VMEM)
    smem = pl.BlockSpec(memory_space=pltpu.SMEM)
    hbm = pl.BlockSpec(memory_space=pl.ANY)
    dma = pltpu.SemaphoreType.DMA
    scratch = [
        pltpu.VMEM((KV, SEQ, QB, HEAD), BF16),
        pltpu.VMEM((PREFIX, KV * HEAD), BF16),
        pltpu.VMEM((KV, PREFIX, 2 * HEAD), BF16),
        pltpu.VMEM((SEQ, MSG, HEAD), BF16),
        pltpu.VMEM((SEQ, MSG, HEAD), BF16),
        pltpu.VMEM((HEADS, ROWS, HEAD), F32),
        pltpu.VMEM((ROWS, 128), F32),
        pltpu.VMEM((PAIR, QUARTER // 2), BF16),
        pltpu.VMEM((4, PAIR, QUARTER // 2), BF16),
        pltpu.VMEM((2, TOTAL, EXT), BF16),
        pltpu.VMEM((WIDTH, UNITS), BF16),
        pltpu.VMEM((WIDTH, UNITS), BF16),
        pltpu.VMEM((UNITS, WIDTH), BF16),
        pltpu.VMEM((1024, UNITS), BF16),
        pltpu.VMEM((128, HALF), BF16),
        pltpu.VMEM((TOTAL, UNITS), F32),
        pltpu.VMEM((TOTAL, UNITS), F32),
        pltpu.VMEM((TOTAL, EXT), BF16),
        pltpu.VMEM((TOTAL, EXT), BF16),
        pltpu.VMEM((TOTAL, EXT), F32),
        pltpu.VMEM((4, 4, PAIR, EXT), BF16),
        pltpu.VMEM((4, 4, PAIR, CUT), BF16),
        pltpu.VMEM((4, 4, PAIR, EXT - CUT), BF16),
        pltpu.VMEM((4, PAIR, CUT), BF16),
        pltpu.VMEM((4, PAIR, EXT - CUT), BF16),
        pltpu.VMEM((4, PAIR, CUT), BF16),
        pltpu.VMEM((4, PAIR, EXT - CUT), BF16),
        pltpu.VMEM((4, PAIR, QUARTER // 2), BF16),
        pltpu.VMEM((EXP, PAIR, QUARTER // 2), BF16),
        pltpu.VMEM((ROWS, QUARTER), F32),
        dma((9,)),
        dma((CHIPS,)),
        dma((CHIPS,)),
        dma((SEQ,)),
        dma((SEQ,)),
        dma((SEQ,)),
        dma((EXP,)),
        dma((4,)),
        dma((CHIPS,)),
        dma((CHIPS,)),
        dma((2, CHIPS)),
        dma((1,)),
        dma((1,)),
        dma((4,)),
        dma((4,)),
    ] + [dma((4,)) for _ in range(10)]
    return pl.pallas_call(
        kernel,
        out_shape=jax.ShapeDtypeStruct((ROWS, QUARTER), BF16),
        in_specs=[vmem, vmem, vmem, vmem, hbm, hbm, vmem, vmem, hbm, hbm, hbm, hbm, hbm, smem, smem, smem],
        out_specs=vmem,
        scratch_shapes=scratch,
        compiler_params=pltpu.CompilerParams(
            collective_id=0, has_side_effects=True, vmem_limit_bytes=58 * 1024 * 1024
        ),
        cost_estimate=pl.CostEstimate(flops=5 * 10**9, bytes_accessed=13 * 2**20, transcendentals=7 * 10**6),
        name="layer",
    )(
        hidden, queries, suffix_row_keys, suffix_row_values, prefix_cached_keys,
        prefix_cached_values, expert_norm_gain.reshape(1, WIDTH), router.T,
        gate_weight.reshape(WIDTH, UNITS), up_weight.reshape(WIDTH, UNITS),
        down_weight.reshape(UNITS, WIDTH), adapter_down_maps.reshape(-1, UNITS),
        adapter_up_maps.reshape(-1, WIDTH), routes.T, tenants, lengths,
    )


def solution(mesh):
    in_specs = (
        P("seq", "exp"),
        P("seq", "exp"),
        P("seq", "exp"),
        P("seq", "exp"),
        P("seq", "exp"),
        P("seq", "exp"),
        P(),
        P(),
        P("exp", None, "seq"),
        P("exp", None, "seq"),
        P("exp", "seq", None),
        P(None, "exp", None, "seq"),
        P("seq", "exp", None, None),
        P(),
        P(),
        P(),
    )
    return jax.shard_map(
        on_device, mesh=mesh, in_specs=in_specs, out_specs=P("seq", "exp"), check_vma=False
    )
```

time: 753 us -> 102 us (0.14)
  local copies, waits for them, and re-layouts: 198 us -> 2.68 us
  blocking collectives: 195 us -> 0 us
  waiting for transfers between devices: 180 us -> 0 us
  other arithmetic: 127 us -> 0 us
  Pallas kernels: 0 us -> 97.9 us
  matrix products: 32.9 us -> 0 us
  between operations: 14.1 us -> 0.01 us
    all_gather x2 -> x0, waiting for transfers between devices: 161 us -> none  [the longest x1 101 us: merged(): everything = jax.tree.map(lambda part: lax.all_gather(part, axis), x)]
    unnamed x1 -> x0, blocking collectives: 121 us -> none
    pallas_call x0 -> x1, Pallas kernels: none -> 97.9 us  [on_device(): pl.pallas_call(kernel, out_shape=jax.ShapeDtypeStruct((ROWS, QUARTER), BF...]
    add x65 -> x0, other arithmetic: 88.2 us -> none  [the longest x31 86.5 us: combine_parts(): earlier_part[2] * scale_early[..., None]]
    dynamic_slice x63 -> x0, local copies, waits for them, and re-layouts: 81.6 us -> none  [the longest x62 81.5 us: step(): return combine(so_far, jax.tree.map(lambda part: part[k], everything))]
    all_gather x3 -> x0, blocking collectives: 74 us -> none  [the longest x2 47.2 us: merged(): everything = jax.tree.map(lambda part: lax.all_gather(part, axis), x)]
    while x139 -> x0, local copies, waits for them, and re-layouts: 54.8 us -> none
    dot_general x22 -> x0, matrix products: 32.9 us -> none  [the longest x6 11.3 us: one_block(): lax.dot_general(query_block, key_rows, (((1,), (1,)), ((), ())), preferre...]
  transfers between devices with their start and end apart: 4 -> 0, of which waited for: 3 -> 0; matrix products, arithmetic and copies ran while one was open for 3% -> 0% of each run, Pallas kernels for 0% -> 0%
where the time goes in v1:
time: 102 us; the launch traced here: 101 us
  Pallas kernels  97.9 us (96%)
  local copies, waits for them, and re-layouts  2.68 us (3%)
    pallas_call x1, Pallas kernels, on_device(): pl.pallas_call(kernel, out_shape=jax.ShapeDtypeStruct((ROWS, QUARTER), BF...  97.9 us

profile of v1, /device:TPU:1, one launch (start us, length us, event | category | flops | bytes accessed | tf_op | source)
XLA Modules:
  0.0 100.6 jit_solution(9333732612158838077)
XLA Ops:
  0.0 1.3 %reshape.18.gain = bf16[1,6144]{1,0:T(2,128)(2,1)} reshape(bf16[6144]{0:T(1024)(128)(2,1)} %param.22) | data formatting | bytes 24576 | tf_op jit(solution)/shard_map/reshape | solution.py:651
  1.3 97.9 %layer.1 = bf16[8,1536]{1,0:T(8,128)(2,1)} custom-call(bf16[8,1536]{1,0:T(8,128)(2,1)} %hid.1, bf16[8,1536]{1,0:T(8,128)(2,1)} %qry.1, bf16[8,256]{1,0:T(8,128)(2,1)} %skey.1, bf16[8,256]{1,0:T(8,128)(2,1)} %sval.1, bf16[2048,256]{1,0:T(8,128)(2,1)} %pk.1, bf16[2048,256]{1,0:T(8,128)(2,1)} %pv.1, bf16[1,6144]{1,0:T(2,128)(2,1)} %reshape.18.gain, ...), custom_call_target="tpu_custom_call" | custom-call | flops 5000000000 | bytes 13631488 | tf_op jit(solution)/shard_map/layer/pallas_call | solution.py:638
  99.3 1.3 %copy.18 = bf16[8,1536]{1,0:T(8,128)(2,1)} copy(bf16[8,1536]{1,0:T(8,128)(2,1)} %layer.1) | data formatting | bytes 49152

commit v2 on v1

v2 whole, which is shorter than its diff:
```python
import functools

import jax
import jax.numpy as jnp
from jax import lax
from jax.experimental import pallas as pl
from jax.experimental.pallas import tpu as pltpu
from jax.sharding import PartitionSpec as P

MESH = pl.DeviceIdType.MESH
F32 = jnp.float32
BF16 = jnp.bfloat16

HEAD = 128
GROUP = 6
KV = 2
HEADS = KV * GROUP
ROWS = 8
SEQ = 32
EXP = 4
CHIPS = SEQ // 2
PAIR = 2 * ROWS
TOTAL = SEQ * ROWS
WIDTH = 6144
HALF = WIDTH // 2
QUARTER = WIDTH // EXP
PREFIX = 2048
UNITS = 256
QB = GROUP * ROWS
BLK = 2 * QB
MSG = BLK + 16
PART = GROUP * HEAD
THIRD = PART // 3
KEYS = 512
EXT = HALF + 128
CUT = 1536
NORM_EPS = 1e-05
LOG2E = 1.4426950408889634
SCALE2 = HEAD**-0.5 * LOG2E


def dot(a, b):
    return jnp.dot(a, b, preferred_element_type=F32)


def dot_t(a, b):
    return lax.dot_general(a, b, (((1,), (1,)), ((), ())), preferred_element_type=F32)


def iota(shape, dim):
    return lax.broadcasted_iota(jnp.int32, shape, dim)


def three_parts(v):
    high = v.astype(BF16).astype(F32)
    rest = v - high
    mid = rest.astype(BF16).astype(F32)
    low = rest - mid
    ax = v.ndim - 1
    return high + pltpu.roll(mid, 16, ax) + pltpu.roll(low, 32, ax)


def whole_of(p):
    ax = p.ndim - 1
    return p + pltpu.roll(p, 128 - 16, ax) + pltpu.roll(p, 128 - 32, ax)


N_SMALL = 6


def kernel(
    hid, qry, skey, sval, pk, pv, gain, rout, wg, wu, wd, adn, aup, routes, tenants, lengths,
    out,
    hid_v, qry_v, skey_v, sval_v, rout_v, gain_v, gainf, msnd, pairb, qall, kbuf, vext, sbuf, pbuf,
    suf_o, suf_l, xb, wgb, wub, wdb, adnb, upb,
    accg, accu, accs, s1snd, s1rcv, own, p2, r2a, r2b, p3a, p3b, r3a, r3b, fsnd, fbuf,
    lsem, ms, mr, ks, kr, qs, qr, ps, pr, gs, gr, hs, hr, ups, upr, s1s, s1r,
    as2, ar2, bs2, br2, as3, ar3, bs3, br3, fs, fr,
):
    s = lax.axis_index("seq")
    z = lax.axis_index("exp")
    k = lax.rem(s, 2)
    c = lax.div(s, 2)
    x = lax.rem(c, 4)
    y = lax.div(c, 4)
    sib = s + 1 - 2 * k
    sent = []

    def remote(src, dst, ssem, rsem, seq, exp):
        return pltpu.make_async_remote_copy(
            src_ref=src, dst_ref=dst, send_sem=ssem, recv_sem=rsem,
            device_id=(seq, exp), device_id_type=MESH,
        )

    def each(n, body, first=0):
        def step(i, carry):
            body(i)
            return carry

        lax.fori_loop(first, n, step, 0)

    def chip_at(i):
        return lax.rem(y + 4 - i // 4, 4) * 4 + lax.rem(x + i % 4, 4)

    barrier = pltpu.get_barrier_semaphore()

    def greet(seq, exp):
        pl.semaphore_signal(barrier, inc=1, device_id=(seq, exp), device_id_type=MESH)

    greet(sib, z)
    each(CHIPS, lambda i: greet(chip_at(i) * 2 + k, z), 1)
    for d in range(1, EXP):
        for seq in (s, sib):
            greet(seq, lax.rem(z + d, EXP))

    k_half = pl.multiple_of(k * HALF, HALF)
    own_head = pl.ds(pl.multiple_of(k * HEAD, HEAD), HEAD)
    sib_head = pl.ds(pl.multiple_of(HEAD - k * HEAD, HEAD), HEAD)
    up_row = pl.multiple_of(64 * lax.rem(c, 2) + 32 * k, 32)
    loads = [
        (qry, qry_v),
        (hid, hid_v),
        (skey, skey_v),
        (sval, sval_v),
        (gain, gain_v),
        (rout, rout_v),
        (pk.at[:, own_head], kbuf.at[pl.ds(0, PREFIX), :]),
        (pv.at[:, own_head], vext.at[pl.ds(0, PREFIX), pl.ds(0, HEAD)]),
        (wg, wgb),
        (wu, wub),
        (wd, wdb),
        (adn, adnb),
        (aup.at[:, pl.ds(k_half, HALF)], upb.at[pl.ds(up_row, 32), :]),
    ]
    loads = [pltpu.make_async_copy(a, b, lsem.at[i]) for i, (a, b) in enumerate(loads)]
    for cp in loads:
        cp.start()
    vext[:, HEAD:] = jnp.ones((2 * PREFIX, HEAD), BF16)
    other_rows = pl.multiple_of(64 - 64 * lax.rem(c, 2), 64)
    upb[pl.ds(other_rows, 64), :] = jnp.zeros((64, HALF), BF16)
    for cp in loads[:N_SMALL]:
        cp.wait()
    gainf[...] = gain_v[...].astype(F32).reshape(1, WIDTH)

    q, h = qry_v[...].astype(F32), hid_v[...].astype(F32)
    kv = [skey_v[...].astype(F32), sval_v[...].astype(F32)]
    by_head = []
    for g in range(KV):
        tiles = [a[:, (g * GROUP + j) * HEAD : (g * GROUP + j + 1) * HEAD] for a in (q, h) for j in range(GROUP)]
        tiles = tiles + [a[:, g * HEAD : (g + 1) * HEAD] for a in kv]
        by_head.append(jnp.concatenate(tiles, axis=0))
    pairb[k] = jnp.where(k == 0, by_head[0], by_head[1]).astype(BF16)
    msnd[...] = jnp.where(k == 0, by_head[1], by_head[0]).astype(BF16)
    pl.semaphore_wait(barrier, CHIPS + 2 * (EXP - 1))

    m_copy = remote(msnd, pairb.at[k], ms.at[0], mr.at[0], sib, z)
    m_copy.start()
    kv_copies = [
        remote(pk.at[:, sib_head], kbuf.at[pl.ds(PREFIX, PREFIX), :], ks.at[0], kr.at[0], sib, z),
        remote(pv.at[:, sib_head], vext.at[pl.ds(PREFIX, PREFIX), pl.ds(0, HEAD)], ks.at[1], kr.at[1], sib, z),
    ]
    for cp in kv_copies:
        cp.start()
    sent.append(lambda: [cp.wait_send() for cp in (m_copy, *kv_copies)])
    remote(msnd, pairb.at[1 - k], ms.at[0], mr.at[0], sib, z).wait_recv()

    for kk in range(2):
        qall[c, kk * QB : (kk + 1) * QB, :] = pairb[kk, 0:QB, :]

    def q_send(i):
        return remote(qall.at[c], qall.at[c], qs.at[i], qr.at[c], chip_at(i) * 2 + k, z)

    each(CHIPS, lambda i: q_send(i).start(), 1)
    sent.append(lambda: each(CHIPS, lambda i: q_send(i).wait_send(), 1))
    up_other = pl.multiple_of(HALF - k * HALF, HALF)

    def up_copy():
        return remote(
            aup.at[:, pl.ds(up_other, HALF)], upb.at[pl.ds(up_row, 32), :], ups.at[0], upr.at[0], sib, z
        )

    up_copy().start()
    sent.append(lambda: up_copy().wait_send())

    row16 = iota((PAIR, 128), 0)
    lane16 = iota((PAIR, 128), 1)
    ten = [tenants[c * PAIR + i] for i in range(PAIR)]
    pos = []
    for i in range(PAIR):
        p = jnp.int32(0)
        for j in range(i // ROWS * ROWS, i):
            p = p + (ten[i] == ten[j]).astype(jnp.int32)
        pos.append(p)
    lens = [lengths[t] for t in ten]

    def spread(values, at):
        got = jnp.full((PAIR, 128), -1, jnp.int32)
        for i, v in enumerate(values):
            got = jnp.where(at == i, v, got)
        return got

    ten_rows = spread(ten, row16)
    pos_c = spread(pos, lane16)
    visible = (lane16 < PAIR) & (ten_rows == spread(ten, lane16))
    visible = visible & (pos_c <= spread(pos, row16)) & (pos_c < spread(lens, row16))
    pairs = [pairb[kk, BLK:, :].astype(F32) for kk in range(2)]
    fill = jnp.zeros((128 - PAIR, HEAD), F32)
    keys = jnp.concatenate([pairs[0][:ROWS], pairs[1][:ROWS], fill], axis=0).astype(BF16)
    values = jnp.concatenate([pairs[0][ROWS:], pairs[1][ROWS:], fill], axis=0).astype(BF16)
    for kk in range(2):
        seen = visible[kk * ROWS : (kk + 1) * ROWS]
        seen = jnp.broadcast_to(seen[None], (GROUP, ROWS, 128))
        sc = dot_t(pairb[kk, 0:QB, :], keys).reshape(GROUP, ROWS, 128)
        sc = jnp.where(seen, sc, -1e30)
        m = jnp.max(sc, axis=2, keepdims=True)
        w = jnp.where(seen, jnp.exp2((sc - m) * SCALE2), 0.0)
        mass = jnp.sum(w, axis=2, keepdims=True)
        acc = dot(w.reshape(QB, 128).astype(BF16), values).reshape(GROUP, ROWS, HEAD)
        suf_o[kk] = acc / mass
        lse = jnp.broadcast_to(m * SCALE2 + jnp.log2(mass), (GROUP, ROWS, 128))
        stat = jnp.zeros((ROWS, 128), F32)
        for j in range(GROUP):
            stat = jnp.where(lane16[:ROWS] == j, lse[j], stat)
        suf_l[kk * ROWS : (kk + 1) * ROWS, :] = stat

    for cp in loads[N_SMALL : N_SMALL + 2]:
        cp.wait()
    for cp in kv_copies:
        cp.wait_recv()

    def p_copy(chip):
        return remote(sbuf.at[chip], pbuf.at[c], ps.at[chip], pr.at[c], chip * 2 + k, z)

    def attend(dy):
        yy = lax.rem(y + dy, 4)

        def q_wait(i):
            chip = yy * 4 + i

            @pl.when(chip != c)
            def _():
                remote(qall.at[c], qall.at[chip], qs.at[0], qr.at[chip], chip * 2 + k, z).wait_recv()

        each(4, q_wait)
        qs_ = qall[pl.ds(yy * 4, 4)].reshape(4 * BLK, HEAD)
        coming = dot_t(qs_, kbuf[0:KEYS, :])
        m = acc = None
        for at in range(0, 2 * PREFIX, KEYS):
            sc = coming * SCALE2
            if at + KEYS < 2 * PREFIX:
                coming = dot_t(qs_, kbuf[at + KEYS : at + 2 * KEYS, :])
            top = jnp.max(sc, axis=1, keepdims=True)
            top = top if m is None else jnp.maximum(m, top)
            got = dot(jnp.exp2(sc - top).astype(BF16), vext[at : at + KEYS, :])
            acc = got if m is None else acc * jnp.exp2(m - top) + got
            m = top
        mass = acc[:, HEAD:]
        o = acc[:, :HEAD] / mass
        sbuf[pl.ds(yy * 4, 4), 0:BLK, :] = o.astype(BF16).reshape(4, BLK, HEAD)
        lse = (m + jnp.log2(mass)).reshape(8, GROUP, ROWS, 128)
        lane = iota((8, ROWS, 128), 2)
        stat = jnp.zeros((8, ROWS, 128), F32)
        for j in range(GROUP):
            stat = jnp.where(lane == j, lse[:, j], stat)
        sbuf[pl.ds(yy * 4, 4), BLK:, :] = three_parts(stat).reshape(4, PAIR, 128).astype(BF16)

        def p_send(i):
            chip = yy * 4 + lax.rem(x + i, 4)

            @pl.when(chip != c)
            def _():
                p_copy(chip).start()

        each(4, p_send)

    each(4, attend)

    def partials_sent():
        def one(i):
            @pl.when(i != c)
            def _():
                p_copy(i).wait_send()

        each(CHIPS, one)

    sent.append(partials_sent)
    pbuf[c] = sbuf[c]

    def p_wait(i):
        @pl.when(i != c)
        def _():
            remote(sbuf.at[i], pbuf.at[i], ps.at[i], pr.at[i], i * 2 + k, z).wait_recv()

    each(CHIPS, p_wait)
    lses = whole_of(pbuf[:, BLK:, :].astype(F32))
    top = jnp.maximum(jnp.max(lses, axis=0), suf_l[...])
    shares = jnp.exp2(lses - top[None])
    suf_share = jnp.exp2(suf_l[...] - top)
    inverse = 1.0 / (jnp.sum(shares, axis=0) + suf_share)
    suf_share = suf_share * inverse
    att = {}
    for kk in range(2):
        rows = slice(kk * ROWS, (kk + 1) * ROWS)
        hidden = pairb[kk, QB : 2 * QB, :].astype(F32)
        for j in range(GROUP):
            att[kk, j] = hidden[j * ROWS : (j + 1) * ROWS] + suf_share[rows, j : j + 1] * suf_o[kk, j]
    for i in range(CHIPS):
        part = pbuf[i, 0:BLK, :].astype(F32)
        share = shares[i] * inverse
        for kk in range(2):
            rows = slice(kk * ROWS, (kk + 1) * ROWS)
            for j in range(GROUP):
                at = (kk * GROUP + j) * ROWS
                att[kk, j] = att[kk, j] + share[rows, j : j + 1] * part[at : at + ROWS]
    resid = [jnp.concatenate([att[kk, j] for j in range(GROUP)], axis=1) for kk in range(2)]
    xb[k, z, y, x] = jnp.concatenate(resid, axis=0).astype(BF16)

    here = {"x": x, "y": y, "z": z}
    orders = ("xyz", "yzx", "zxy")

    def region(t, step, **at):
        at = {**here, **at}
        index = [pl.ds(0, 4) if a in orders[t][:step] else at[a] for a in "zyx"]
        return xb.at[(k, *index, slice(None), pl.ds(t * THIRD, THIRD))]

    def peer(axis, d):
        at = {**here, axis: lax.rem(here[axis] + d, 4)}
        return at[axis], (at["y"] * 4 + at["x"]) * 2 + k, at["z"]

    def g_send(t, step, d):
        axis = orders[t][step]
        _, seq, exp = peer(axis, d)
        block = region(t, step)
        return remote(block, block, gs.at[t, step, d], gr.at[t, step, here[axis]], seq, exp)

    def g_wait(t, step, d):
        axis = orders[t][step]
        there, seq, exp = peer(axis, d)
        block = region(t, step, **{axis: there})
        remote(block, block, gs.at[t, step, 0], gr.at[t, step, there], seq, exp).wait_recv()

    def h_copy(t, there):
        block = region(t, 2, **{orders[t][2]: there})
        return remote(block, block, hs.at[t, there], hr.at[t, there], sib, z)

    for step in range(3):
        for t in range(3):
            if step:
                for d in (1, 3, 2):
                    g_wait(t, step - 1, d)
            for d in (2, 1, 3):
                g_send(t, step, d).start()
    for t in range(3):
        h_copy(t, here[orders[t][2]]).start()
    for d in (1, 3, 2):
        for t in range(3):
            g_wait(t, 2, d)
            h_copy(t, peer(orders[t][2], d)[0]).start()

    def rows_sent():
        for t in range(3):
            for step in range(3):
                for d in (1, 2, 3):
                    g_send(t, step, d).wait_send()
            for there in range(4):
                h_copy(t, there).wait_send()

    sent.append(rows_sent)

    for cp in loads[N_SMALL + 2 : N_SMALL + 4]:
        cp.wait()
    accg[...] = jnp.zeros_like(accg)
    accu[...] = jnp.zeros_like(accu)
    accs[...] = jnp.zeros_like(accs)

    def project(core):
        def one(zz):
            at = pl.multiple_of(zz * QUARTER + core * PART, PART)
            rows = xb[core, zz].reshape(TOTAL, PART).astype(F32)
            squares = rows * rows
            total = squares[:, 0:128]
            for i in range(1, PART // 128):
                total = total + squares[:, i * 128 : (i + 1) * 128]
            accs[...] = accs[...] + total
            rows = (rows * gainf[:, pl.ds(at, PART)]).astype(BF16)
            accg[...] = accg[...] + dot(rows, wgb[pl.ds(at, PART), :])
            accu[...] = accu[...] + dot(rows, wub[pl.ds(at, PART), :])

        each(EXP, one)

    project(k)
    for t in range(3):
        for there in range(4):
            block = xb.at[(1 - k, *[there if a == orders[t][2] else pl.ds(0, 4) for a in "zyx"], slice(None), pl.ds(t * THIRD, THIRD))]
            remote(block, block, hs.at[t, there], hr.at[t, there], sib, z).wait_recv()
    project(1 - k)
    scale = lax.rsqrt(jnp.sum(accs[...], axis=1, keepdims=True) / WIDTH + NORM_EPS)
    gate = accg[...] * scale
    units = (gate / (1.0 + jnp.exp(-gate)) * (accu[...] * scale)).astype(BF16)

    for cp in loads[N_SMALL + 4 :]:
        cp.wait()
    low = [
        dot_t(units[i * 32 : (i + 1) * 32], adnb[i * 128 : (i + 1) * 128, :])
        for i in range(CHIPS // 2)
    ]
    low = jnp.concatenate(low, axis=0)
    s1snd[:, HALF:] = low.astype(BF16)
    own[:, HALF:] = low

    part = 768
    n_parts = HALF // part
    widths = [part] * (n_parts - 1) + [part + 128]

    def s1_copy(i):
        at = pl.ds(i * part, widths[i])
        return remote(s1snd.at[:, at], s1rcv.at[:, at], s1s.at[i], s1r.at[i], sib, z)

    def down(half, i):
        at = pl.multiple_of(half * HALF + i * part, 128)
        return dot(units, wdb[:, pl.ds(at, part)])

    for i in range(n_parts):
        s1snd[:, i * part : (i + 1) * part] = down(1 - k, i).astype(BF16)
        s1_copy(i).start()
    for i in range(n_parts):
        own[:, i * part : (i + 1) * part] = down(k, i)
    sent.append(lambda: [s1_copy(i).wait_send() for i in range(n_parts)])

    def a2_copy(d):
        xx = lax.rem(x + d, 4)
        return remote(
            p2.at[:, xx, :, pl.ds(0, CUT)], r2a.at[x], as2.at[d], ar2.at[x], (y * 4 + xx) * 2 + k, z
        )

    def b2_copy(d):
        yy = lax.rem(y + d, 4)
        return remote(
            p2.at[yy, :, :, pl.ds(CUT, EXT - CUT)], r2b.at[y], bs2.at[d], br2.at[y],
            (yy * 4 + x) * 2 + k, z,
        )

    for i in range(n_parts):
        s1_copy(i).wait_recv()
        at = slice(i * part, i * part + widths[i])
        both = own[:, at] + s1rcv[:, at].astype(F32)
        p2[:, :, :, at] = both.astype(BF16).reshape(4, 4, PAIR, widths[i])
        if (i + 1) * part == CUT:
            for d in (2, 1, 3):
                a2_copy(d).start()
    for d in (2, 1, 3):
        b2_copy(d).start()
    sent.append(lambda: [copy(d).wait_send() for copy in (a2_copy, b2_copy) for d in (2, 1, 3)])

    def column(load):
        got = jnp.zeros((PAIR, 128), jnp.int32)
        for i in range(PAIR):
            got = jnp.where(row16 == i, load(c * PAIR + i), got)
        return got

    first = column(lambda i: routes[0, i])
    second = column(lambda i: routes[1, i])
    other = first + second - z
    logits = [jnp.zeros((PAIR, 1), F32)] * EXP
    squares = jnp.zeros((PAIR, 1), F32)
    for kk in range(2):
        for zz in range(EXP):
            at = slice(zz * QUARTER + kk * PART, zz * QUARTER + (kk + 1) * PART)
            rows = xb[kk, zz, y, x].astype(F32)
            squares = squares + jnp.sum(rows * rows, axis=1, keepdims=True)
            rows = (rows * gainf[:, at]).astype(BF16).astype(F32)
            for e in range(EXP):
                by = rout_v[e : e + 1, at].astype(F32)
                logits[e] = logits[e] + jnp.sum(rows * by, axis=1, keepdims=True)
    own_scale = lax.rsqrt(squares / WIDTH + NORM_EPS)
    mine = jnp.zeros((PAIR, 128), F32)
    theirs = jnp.zeros((PAIR, 128), F32)
    for e in range(EXP):
        logit = logits[e] * own_scale
        mine = jnp.where(z == e, logit, mine)
        theirs = jnp.where(other == e, logit, theirs)
    share = 1.0 / (1.0 + jnp.exp(theirs - mine))
    share = jnp.where((first == z) | (second == z), share, 0.0)[:, 0:1]

    def a2_wait(d):
        xx = lax.rem(x + d, 4)
        remote(
            p2.at[:, x, :, pl.ds(0, CUT)], r2a.at[xx], as2.at[0], ar2.at[xx],
            (y * 4 + xx) * 2 + k, z,
        ).wait_recv()
        return xx

    def b2_wait(d):
        yy = lax.rem(y + d, 4)
        remote(
            p2.at[y, :, :, pl.ds(CUT, EXT - CUT)], r2b.at[yy], bs2.at[0], br2.at[yy],
            (yy * 4 + x) * 2 + k, z,
        ).wait_recv()
        return yy

    total = p2[:, x, :, 0:CUT].astype(F32)
    for d in (1, 3, 2):
        total = total + r2a[a2_wait(d)].astype(F32)
    p3a[...] = total.astype(BF16)

    def a3_copy(d):
        yy = lax.rem(y + d, 4)
        return remote(p3a.at[yy], r3a.at[y], as3.at[d], ar3.at[y], (yy * 4 + x) * 2 + k, z)

    for d in (2, 1, 3):
        a3_copy(d).start()
    total = p2[y, :, :, CUT:].astype(F32)
    for d in (1, 3, 2):
        total = total + r2b[b2_wait(d)].astype(F32)
    p3b[...] = total.astype(BF16)

    def b3_copy(d):
        xx = lax.rem(x + d, 4)
        return remote(p3b.at[xx], r3b.at[x], bs3.at[d], br3.at[x], (y * 4 + xx) * 2 + k, z)

    for d in (2, 1, 3):
        b3_copy(d).start()
    sent.append(lambda: [copy(d).wait_send() for copy in (a3_copy, b3_copy) for d in (2, 1, 3)])

    sum_a = p3a[y].astype(F32)
    for d in (1, 3, 2):
        yy = lax.rem(y + d, 4)
        remote(p3a.at[y], r3a.at[yy], as3.at[0], ar3.at[yy], (yy * 4 + x) * 2 + k, z).wait_recv()
        sum_a = sum_a + r3a[yy].astype(F32)
    sum_b = p3b[x].astype(F32)
    for d in (1, 3, 2):
        xx = lax.rem(x + d, 4)
        remote(p3b.at[x], r3b.at[xx], bs3.at[0], br3.at[xx], (y * 4 + xx) * 2 + k, z).wait_recv()
        sum_b = sum_b + r3b[xx].astype(F32)

    up_copy().wait_recv()
    low = sum_b[:, HALF - CUT :]
    low = jnp.where(lax.div(iota((PAIR, 128), 1), 16) == lax.rem(ten_rows, 8), low, 0.0)
    adapter = dot(low.astype(BF16), upb[...])
    contrib = (jnp.concatenate([sum_a, sum_b[:, : HALF - CUT]], axis=1) + adapter) * share

    def f_copy(kk, j):
        slot = kk * 2 + j
        return remote(fsnd.at[slot], fbuf.at[z], fs.at[slot], fr.at[z], c * 2 + kk, 2 * k + j)

    for kk in range(2):
        for j in range(2):
            slot = kk * 2 + j
            rows = contrib[kk * ROWS : (kk + 1) * ROWS, j * QUARTER : (j + 1) * QUARTER]
            fsnd[slot] = jnp.concatenate([rows[:, :PART], rows[:, PART:]], axis=0).astype(BF16)
            is_self = (kk == k) & (2 * k + j == z)

            @pl.when(~is_self)
            def _():
                f_copy(kk, j).start()

            @pl.when(is_self)
            def _():
                fbuf[z] = fsnd[slot]

    to_core = lax.div(z, 2)
    for e in range(EXP):

        @pl.when(~((to_core == k) & (e == z)))
        def _():
            remote(fsnd.at[0], fbuf.at[e], fs.at[0], fr.at[e], c * 2 + to_core, e).wait_recv()

    def final_sent():
        for kk in range(2):
            for j in range(2):

                @pl.when(~((kk == k) & (2 * k + j == z)))
                def _():
                    f_copy(kk, j).wait_send()

    sent.append(final_sent)
    got = fbuf[...].astype(F32)
    got = got[0] + got[1] + got[2] + got[3]
    got = jnp.concatenate([got[:ROWS], got[ROWS:]], axis=1)
    resid = [xb[kk, z, y, x].astype(F32) for kk in range(2)]
    resid = [jnp.where(k == 0, r[:ROWS], r[ROWS:]) for r in resid]
    out[...] = (jnp.concatenate(resid, axis=1) + got).astype(BF16)

    for wait in sent:
        wait()


def on_device(
    hidden, queries, suffix_row_keys, suffix_row_values, prefix_cached_keys, prefix_cached_values,
    expert_norm_gain, router, gate_weight, up_weight, down_weight, adapter_down_maps,
    adapter_up_maps, routes, tenants, lengths,
):
    vmem = pl.BlockSpec(memory_space=pltpu.VMEM)
    smem = pl.BlockSpec(memory_space=pltpu.SMEM)
    hbm = pl.BlockSpec(memory_space=pl.ANY)
    dma = pltpu.SemaphoreType.DMA
    scratch = [
        pltpu.VMEM((ROWS, QUARTER), BF16),
        pltpu.VMEM((ROWS, QUARTER), BF16),
        pltpu.VMEM((ROWS, KV * HEAD), BF16),
        pltpu.VMEM((ROWS, KV * HEAD), BF16),
        pltpu.VMEM((EXP, WIDTH), BF16),
        pltpu.VMEM((WIDTH,), BF16),
        pltpu.VMEM((1, WIDTH), F32),
        pltpu.VMEM((MSG, HEAD), BF16),
        pltpu.VMEM((2, MSG, HEAD), BF16),
        pltpu.VMEM((CHIPS, BLK, HEAD), BF16),
        pltpu.VMEM((2 * PREFIX, HEAD), BF16),
        pltpu.VMEM((2 * PREFIX, 2 * HEAD), BF16),
        pltpu.VMEM((CHIPS, MSG, HEAD), BF16),
        pltpu.VMEM((CHIPS, MSG, HEAD), BF16),
        pltpu.VMEM((2, GROUP, ROWS, HEAD), F32),
        pltpu.VMEM((PAIR, 128), F32),
        pltpu.VMEM((2, EXP, 4, 4, PAIR, PART), BF16),
        pltpu.VMEM((WIDTH, UNITS), BF16),
        pltpu.VMEM((WIDTH, UNITS), BF16),
        pltpu.VMEM((UNITS, WIDTH), BF16),
        pltpu.VMEM((1024, UNITS), BF16),
        pltpu.VMEM((128, HALF), BF16),
        pltpu.VMEM((TOTAL, UNITS), F32),
        pltpu.VMEM((TOTAL, UNITS), F32),
        pltpu.VMEM((TOTAL, 128), F32),
        pltpu.VMEM((TOTAL, EXT), BF16),
        pltpu.VMEM((TOTAL, EXT), BF16),
        pltpu.VMEM((TOTAL, EXT), F32),
        pltpu.VMEM((4, 4, PAIR, EXT), BF16),
        pltpu.VMEM((4, 4, PAIR, CUT), BF16),
        pltpu.VMEM((4, 4, PAIR, EXT - CUT), BF16),
        pltpu.VMEM((4, PAIR, CUT), BF16),
        pltpu.VMEM((4, PAIR, EXT - CUT), BF16),
        pltpu.VMEM((4, PAIR, CUT), BF16),
        pltpu.VMEM((4, PAIR, EXT - CUT), BF16),
        pltpu.VMEM((4, PAIR, PART), BF16),
        pltpu.VMEM((EXP, PAIR, PART), BF16),
        dma((13,)),
        dma((1,)),
        dma((1,)),
        dma((2,)),
        dma((2,)),
        dma((CHIPS,)),
        dma((CHIPS,)),
        dma((CHIPS,)),
        dma((CHIPS,)),
        dma((3, 3, 4)),
        dma((3, 3, 4)),
        dma((3, 4)),
        dma((3, 4)),
        dma((1,)),
        dma((1,)),
        dma((4,)),
        dma((4,)),
    ] + [dma((4,)) for _ in range(10)]
    return pl.pallas_call(
        kernel,
        out_shape=jax.ShapeDtypeStruct((ROWS, QUARTER), BF16),
        in_specs=[hbm] * 13 + [smem] * 3,
        out_specs=vmem,
        scratch_shapes=scratch,
        compiler_params=pltpu.CompilerParams(
            collective_id=0, has_side_effects=True, vmem_limit_bytes=58 * 1024 * 1024
        ),
        cost_estimate=pl.CostEstimate(flops=5 * 10**9, bytes_accessed=13 * 2**20, transcendentals=7 * 10**6),
        name="layer",
    )(
        hidden, queries, suffix_row_keys, suffix_row_values, prefix_cached_keys,
        prefix_cached_values, expert_norm_gain, router.T,
        gate_weight.reshape(WIDTH, UNITS), up_weight.reshape(WIDTH, UNITS),
        down_weight.reshape(UNITS, WIDTH), adapter_down_maps.reshape(-1, UNITS),
        adapter_up_maps.reshape(-1, WIDTH), routes.T, tenants, lengths,
    )


def solution(mesh):
    in_specs = (
        P("seq", "exp"),
        P("seq", "exp"),
        P("seq", "exp"),
        P("seq", "exp"),
        P("seq", "exp"),
        P("seq", "exp"),
        P(),
        P(),
        P("exp", None, "seq"),
        P("exp", None, "seq"),
        P("exp", "seq", None),
        P(None, "exp", None, "seq"),
        P("seq", "exp", None, None),
        P(),
        P(),
        P(),
    )
    return jax.shard_map(
        on_device, mesh=mesh, in_specs=in_specs, out_specs=P("seq", "exp"), check_vma=False
    )
```

time: 102 us -> 76.4 us (0.75); the launches traced: 101 us -> 76.2 us
  Pallas kernels: 97.9 us -> 74.8 us
  local copies, waits for them, and re-layouts: 2.68 us -> 1.35 us
    pallas_call x1, Pallas kernels: 97.9 us -> 74.8 us  [on_device(): pl.pallas_call(kernel, out_shape=jax.ShapeDtypeStruct((ROWS, QUARTER), BF...]
    reshape x1 -> x0, local copies, waits for them, and re-layouts: 1.33 us -> none  [on_device(): expert_norm_gain.reshape(1, WIDTH)]
where the time goes in v2:
time: 76.4 us; the launch traced here: 76.2 us
  Pallas kernels  74.8 us (98%)
  local copies, waits for them, and re-layouts  1.35 us (2%)
    pallas_call x1, Pallas kernels, on_device(): pl.pallas_call(kernel, out_shape=jax.ShapeDtypeStruct((ROWS, QUARTER), BF...  74.8 us

profile of v2, /device:TPU:1, one launch (start us, length us, event | category | flops | bytes accessed | tf_op | source)
XLA Modules:
  0.0 76.2 jit_solution(10396945175262582509)
XLA Ops:
  0.0 74.8 %layer.1 = bf16[8,1536]{1,0:T(8,128)(2,1)} custom-call(bf16[8,1536]{1,0:T(8,128)(2,1)} %hid.1, bf16[8,1536]{1,0:T(8,128)(2,1)} %qry.1, bf16[8,256]{1,0:T(8,128)(2,1)} %skey.1, bf16[8,256]{1,0:T(8,128)(2,1)} %sval.1, bf16[2048,256]{1,0:T(8,128)(2,1)} %pk.1, bf16[2048,256]{1,0:T(8,128)(2,1)} %pv.1, bf16[6144]{0:T(1024)(128)(2,1)} %gain.1, ...), custom_call_target="tpu_custom_call" | custom-call | flops 5000000000 | bytes 13631488 | tf_op jit(solution)/shard_map/layer/pallas_call | solution.py:653
  74.8 1.3 %copy.18 = bf16[8,1536]{1,0:T(8,128)(2,1)} copy(bf16[8,1536]{1,0:T(8,128)(2,1)} %layer.1) | data formatting | bytes 49152

commit v3 on v2

v3 whole, which is shorter than its diff:
```python
import functools

import jax
import jax.numpy as jnp
from jax import lax
from jax.experimental import pallas as pl
from jax.experimental.pallas import tpu as pltpu
from jax.sharding import PartitionSpec as P

MESH = pl.DeviceIdType.MESH
F32 = jnp.float32
BF16 = jnp.bfloat16

HEAD = 128
GROUP = 6
KV = 2
HEADS = KV * GROUP
ROWS = 8
SEQ = 32
EXP = 4
CHIPS = SEQ // 2
PAIR = 2 * ROWS
TOTAL = SEQ * ROWS
WIDTH = 6144
HALF = WIDTH // 2
QUARTER = WIDTH // EXP
PREFIX = 2048
UNITS = 256
QB = GROUP * ROWS
BLK = 2 * QB
MSG = BLK + 16
PART = GROUP * HEAD
THIRD = PART // 3
KEYS = 512
NORM_EPS = 1e-05
LOG2E = 1.4426950408889634
SCALE2 = HEAD**-0.5 * LOG2E


def dot(a, b):
    return jnp.dot(a, b, preferred_element_type=F32)


def dot_t(a, b):
    return lax.dot_general(a, b, (((1,), (1,)), ((), ())), preferred_element_type=F32)


def iota(shape, dim):
    return lax.broadcasted_iota(jnp.int32, shape, dim)


def three_parts(v):
    high = v.astype(BF16).astype(F32)
    rest = v - high
    mid = rest.astype(BF16).astype(F32)
    low = rest - mid
    ax = v.ndim - 1
    return high + pltpu.roll(mid, 16, ax) + pltpu.roll(low, 32, ax)


def whole_of(p):
    ax = p.ndim - 1
    return p + pltpu.roll(p, 128 - 16, ax) + pltpu.roll(p, 128 - 32, ax)


N_SMALL = 9


def kernel(
    hid, qry, skey, sval, pk, pv, gain, rout, wg, wu, wd, adn, aup, routes, tenants_h, lengths_h,
    out,
    tenants, lengths,
    hid_v, qry_v, skey_v, sval_v, rout_v, routes_v, gain_v, gainf, msnd, pairb, qall, kbuf, vbuf, sbuf, pbuf,
    suf_o, suf_l, ksnd, vsnd, xb, wgb, wub, wdb, adnb, upb,
    accg, accu, accs, accl, rpad, rcol, lsnd, lrcv, lpair, asnd, arcv, usnd, urcv,
    p2, r2, p3, r3, p4, r4, fpair,
    lsem, ms, mr, ks, kr, qs, qr, ps, pr, gs, gr, hs, hr, ups, upr, ls, lr, lps, lpr, as_, ar,
    ds, dr, us, ur, ss, sr, fs, fr,
):
    s = lax.axis_index("seq")
    z = lax.axis_index("exp")
    k = lax.rem(s, 2)
    c = lax.div(s, 2)
    x = lax.rem(c, 4)
    y = lax.div(c, 4)
    sib = s + 1 - 2 * k
    sent = []

    def remote(src, dst, ssem, rsem, seq, exp):
        return pltpu.make_async_remote_copy(
            src_ref=src, dst_ref=dst, send_sem=ssem, recv_sem=rsem,
            device_id=(seq, exp), device_id_type=MESH,
        )

    def each(n, body, first=0):
        def step(i, carry):
            body(i)
            return carry

        lax.fori_loop(first, n, step, 0)

    def chip_at(i):
        return lax.rem(y + i // 4, 4) * 4 + lax.rem(x + i % 4, 4)

    barrier = pltpu.get_barrier_semaphore()

    def greet(seq, exp):
        pl.semaphore_signal(barrier, inc=1, device_id=(seq, exp), device_id_type=MESH)

    greet(sib, z)
    for i in range(1, CHIPS):
        greet(chip_at(i) * 2 + k, z)
    for d in range(1, EXP):
        greet(s, lax.rem(z + d, EXP))

    own_head = pl.ds(pl.multiple_of(k * HEAD, HEAD), HEAD)
    sib_head = pl.ds(pl.multiple_of(HEAD - k * HEAD, HEAD), HEAD)
    up_row = pl.multiple_of(64 * lax.rem(c, 2) + 32 * k, 32)
    def up_part(zz, core):
        at = pl.multiple_of(zz * QUARTER + core * PART, PART)
        return aup.at[:, pl.ds(at, PART)], upb.at[pl.ds(up_row, 32), pl.ds(zz * PART, PART)]

    def down_part(zz, core):
        at = pl.multiple_of(zz * QUARTER + core * PART, PART)
        rows = 0 if core is k else UNITS
        return wd.at[:, pl.ds(at, PART)], wdb.at[pl.ds(rows, UNITS), pl.ds(zz * PART, PART)]

    loads = [
        (qry, qry_v),
        (hid, hid_v),
        (skey, skey_v),
        (sval, sval_v),
        (gain, gain_v),
        (rout, rout_v),
        (routes, routes_v),
        (tenants_h, tenants),
        (lengths_h, lengths),
        (pk.at[:, own_head], kbuf.at[pl.ds(0, PREFIX), :]),
        (pv.at[:, own_head], vbuf.at[pl.ds(0, PREFIX), :]),
        (pk.at[:, sib_head], ksnd),
        (pv.at[:, sib_head], vsnd),
        (wg, wgb),
        (wu, wub),
        (adn, adnb),
    ] + [part(zz, k) for part in (up_part, down_part) for zz in range(EXP)]
    loads = [pltpu.make_async_copy(a, b, lsem.at[i]) for i, (a, b) in enumerate(loads)]
    for cp in loads:
        cp.start()
    other_rows = pl.multiple_of(64 - 64 * lax.rem(c, 2), 64)
    upb[pl.ds(other_rows, 64), :] = jnp.zeros((64, HALF), BF16)
    for cp in loads[:N_SMALL]:
        cp.wait()
    gainf[...] = gain_v[...].astype(F32).reshape(1, WIDTH)

    q, h = qry_v[...].astype(F32), hid_v[...].astype(F32)
    kv = [skey_v[...].astype(F32), sval_v[...].astype(F32)]
    by_head = []
    for g in range(KV):
        tiles = [a[:, (g * GROUP + j) * HEAD : (g * GROUP + j + 1) * HEAD] for a in (q, h) for j in range(GROUP)]
        tiles = tiles + [a[:, g * HEAD : (g + 1) * HEAD] for a in kv]
        by_head.append(jnp.concatenate(tiles, axis=0))
    pairb[k] = jnp.where(k == 0, by_head[0], by_head[1]).astype(BF16)
    msnd[...] = jnp.where(k == 0, by_head[1], by_head[0]).astype(BF16)
    pl.semaphore_wait(barrier, CHIPS + EXP - 1)

    m_copy = remote(msnd, pairb.at[k], ms.at[0], mr.at[0], sib, z)
    m_copy.start()
    kv_copies = [
        remote(ksnd, kbuf.at[pl.ds(PREFIX, PREFIX), :], ks.at[0], kr.at[0], sib, z),
        remote(vsnd, vbuf.at[pl.ds(PREFIX, PREFIX), :], ks.at[1], kr.at[1], sib, z),
    ]
    for cp in loads[N_SMALL + 2 : N_SMALL + 4]:
        cp.wait()
    sent.append(lambda: [cp.wait_send() for cp in (m_copy, *kv_copies)])
    remote(msnd, pairb.at[1 - k], ms.at[0], mr.at[0], sib, z).wait_recv()

    own = [pairb[kk, 0:QB, :] for kk in range(2)]
    qall[c] = jnp.concatenate(own, axis=0)
    order = (1, 2, 3, 12, 13, 14, 15, 8, 9, 10, 11, 4, 5, 6, 7)

    def q_send(i):
        return remote(qall.at[c], qall.at[c], qs.at[i], qr.at[c], chip_at(i) * 2 + k, z)

    for i in order[:3]:
        q_send(i).start()
    kv_copies[0].start()
    for i in order[3:]:
        q_send(i).start()
    kv_copies[1].start()
    sent.append(lambda: [q_send(i).wait_send() for i in order])
    up_copies = []
    for zz in range(EXP):
        src, dst = up_part(zz, 1 - k)
        up_copies.append(remote(src, dst, ups.at[zz], upr.at[zz], sib, z))
    down_copies = []
    for zz in range(EXP):
        src, dst = down_part(zz, 1 - k)
        down_copies.append(remote(src, dst, ds.at[zz], dr.at[zz], sib, z))
    for cp in up_copies + down_copies:
        cp.start()
    sent.append(lambda: [cp.wait_send() for cp in up_copies + down_copies])

    def stacked(rows):
        index = iota((PAIR, rows.shape[1]), 0)
        got = jnp.zeros(index.shape, F32)
        for i in range(rows.shape[0]):
            got = jnp.where(index == i, rows[i : i + 1], got)
        return got.astype(BF16)

    rpad[...] = stacked(rout_v[...].astype(F32))
    eye = (iota((TOTAL, TOTAL), 0) == iota((TOTAL, TOTAL), 1)).astype(F32).astype(BF16)
    rcol[...] = dot_t(eye, stacked(routes_v[...].astype(F32)))

    row16 = iota((PAIR, 128), 0)
    lane16 = iota((PAIR, 128), 1)
    ten = [tenants[c * PAIR + i] for i in range(PAIR)]
    pos = []
    for i in range(PAIR):
        p = jnp.int32(0)
        for j in range(i // ROWS * ROWS, i):
            p = p + (ten[i] == ten[j]).astype(jnp.int32)
        pos.append(p)
    lens = [lengths[t] for t in ten]

    def spread(values, at):
        got = jnp.full((PAIR, 128), -1, jnp.int32)
        for i, v in enumerate(values):
            got = jnp.where(at == i, v, got)
        return got

    ten_rows = spread(ten, row16)
    pos_c = spread(pos, lane16)
    visible = (lane16 < PAIR) & (ten_rows == spread(ten, lane16))
    visible = visible & (pos_c <= spread(pos, row16)) & (pos_c < spread(lens, row16))
    pairs = [pairb[kk, BLK:, :].astype(F32) for kk in range(2)]
    fill = jnp.zeros((128 - PAIR, HEAD), F32)
    keys = jnp.concatenate([pairs[0][:ROWS], pairs[1][:ROWS], fill], axis=0).astype(BF16)
    values = jnp.concatenate([pairs[0][ROWS:], pairs[1][ROWS:], fill], axis=0).astype(BF16)
    for kk in range(2):
        seen = visible[kk * ROWS : (kk + 1) * ROWS]
        seen = jnp.broadcast_to(seen[None], (GROUP, ROWS, 128))
        sc = dot_t(pairb[kk, 0:QB, :], keys).reshape(GROUP, ROWS, 128)
        sc = jnp.where(seen, sc, -1e30)
        m = jnp.max(sc, axis=2, keepdims=True)
        w = jnp.where(seen, jnp.exp2((sc - m) * SCALE2), 0.0)
        mass = jnp.sum(w, axis=2, keepdims=True)
        acc = dot(w.reshape(QB, 128).astype(BF16), values).reshape(GROUP, ROWS, HEAD)
        suf_o[kk] = acc / mass
        lse = jnp.broadcast_to(m * SCALE2 + jnp.log2(mass), (GROUP, ROWS, 128))
        stat = jnp.zeros((ROWS, 128), F32)
        for j in range(GROUP):
            stat = jnp.where(lane16[:ROWS] == j, lse[j], stat)
        suf_l[kk * ROWS : (kk + 1) * ROWS, :] = stat

    for cp in loads[N_SMALL : N_SMALL + 2]:
        cp.wait()
    for cp in kv_copies:
        cp.wait_recv()

    def q_wait(i):
        chip = chip_at(i)
        remote(qall.at[c], qall.at[chip], qs.at[0], qr.at[chip], chip * 2 + k, z).wait_recv()

    tiles = [(u, at) for u in range(4) for at in range(0, 2 * PREFIX, KEYS)]
    queries = {}
    ones = jnp.ones((KEYS, HEAD), BF16)

    def scores(u, at):
        if at == 0:
            for i in range(4 * u, 4 * u + 4):
                if i:
                    q_wait(i)
            queries[u] = qall[pl.ds(lax.rem(y + u, 4) * 4, 4)].reshape(4 * BLK, HEAD)
        return dot_t(queries[u], kbuf[at : at + KEYS, :])

    def finish(u, m, acc):
        mass = acc[:, HEAD:]
        o = (acc[:, :HEAD] / mass).astype(BF16).reshape(4, BLK, HEAD)
        lse = (m + jnp.log2(mass)).reshape(8, GROUP, ROWS, 128)
        lane = iota((8, ROWS, 128), 2)
        stat = jnp.zeros((8, ROWS, 128), F32)
        for j in range(GROUP):
            stat = jnp.where(lane == j, lse[:, j], stat)
        at = pl.ds(lax.rem(y + u, 4) * 4, 4)
        sbuf[at, 0:BLK, :] = o
        sbuf[at, BLK:, :] = three_parts(stat).reshape(4, PAIR, 128).astype(BF16)
        for i in range(4 * u, 4 * u + 4):
            if i:
                p_copy(i).start()

    def p_copy(i):
        chip = chip_at(i)
        return remote(sbuf.at[chip], pbuf.at[c], ps.at[i], pr.at[c], chip * 2 + k, z)

    coming = scores(*tiles[0])
    m = acc = done = None
    for n, (u, at) in enumerate(tiles):
        sc = coming * SCALE2
        if n + 1 < len(tiles):
            coming = scores(*tiles[n + 1])
        if done is not None:
            finish(*done)
            done = None
        top = jnp.max(sc, axis=1, keepdims=True)
        top = top if at == 0 else jnp.maximum(m, top)
        got = dot(jnp.exp2(sc - top).astype(BF16), jnp.concatenate([vbuf[at : at + KEYS, :], ones], axis=1))
        acc = got if at == 0 else acc * jnp.exp2(m - top) + got
        m = top
        if at + KEYS == 2 * PREFIX:
            done = (u, m, acc)
    finish(*done)
    sent.append(lambda: [p_copy(i).wait_send() for i in range(1, CHIPS)])

    pbuf[c] = sbuf[c]
    for i in range(1, CHIPS):
        chip = chip_at(i)
        remote(sbuf.at[chip], pbuf.at[chip], ps.at[0], pr.at[chip], chip * 2 + k, z).wait_recv()
    lses = whole_of(pbuf[:, BLK:, :].astype(F32))
    top = jnp.maximum(jnp.max(lses, axis=0), suf_l[...])
    shares = jnp.exp2(lses - top[None])
    suf_share = jnp.exp2(suf_l[...] - top)
    inverse = 1.0 / (jnp.sum(shares, axis=0) + suf_share)
    suf_share = suf_share * inverse
    att = {}
    for kk in range(2):
        rows = slice(kk * ROWS, (kk + 1) * ROWS)
        hidden = pairb[kk, QB : 2 * QB, :].astype(F32)
        for j in range(GROUP):
            own = suf_share[rows, j : j + 1] * suf_o[kk, j]
            att[kk, j] = hidden[j * ROWS : (j + 1) * ROWS] + own
    for i in range(CHIPS):
        part = pbuf[i, 0:BLK, :].astype(F32)
        share = shares[i] * inverse
        for kk in range(2):
            rows = slice(kk * ROWS, (kk + 1) * ROWS)
            for j in range(GROUP):
                at = (kk * GROUP + j) * ROWS
                att[kk, j] = att[kk, j] + share[rows, j : j + 1] * part[at : at + ROWS]

    here = {"x": x, "y": y, "z": z}
    orders = ("xyz", "yzx", "zxy")

    def region(p, step, core=k, **at):
        at = {**here, **at}
        index = [at[a] for a in orders[p][: step - 1 if step else None : -1]]
        return xb.at[(core, p, *index)]

    def peer(axis, d):
        at = {**here, axis: lax.rem(here[axis] + d, 4)}
        return at[axis], (at["y"] * 4 + at["x"]) * 2 + k, at["z"]

    def g_send(p, step, d):
        axis = orders[p][step]
        _, seq, exp = peer(axis, d)
        block = region(p, step)
        return remote(block, block, gs.at[p, step, d], gr.at[p, step, here[axis]], seq, exp)

    def g_wait(p, step, d):
        axis = orders[p][step]
        there, seq, exp = peer(axis, d)
        block = region(p, step, **{axis: there})
        remote(block, block, gs.at[p, step, 0], gr.at[p, step, there], seq, exp).wait_recv()

    def h_copy(p, there, core):
        block = xb.at[core, p, there]
        return remote(block, block, hs.at[p, there], hr.at[p, there], sib, z)

    def own_block(p, core):
        return (core, p, *[here[a] for a in reversed(orders[p])])

    for p in range(3):
        rows = [jnp.concatenate([att[kk, j] for j in (2 * p, 2 * p + 1)], axis=1) for kk in range(2)]
        xb[own_block(p, k)] = jnp.concatenate(rows, axis=0).astype(BF16)
    for d in (2, 1, 3):
        for p in range(3):
            g_send(p, 0, d).start()
    for step in (1, 2):
        for p in range(3):
            for d in (1, 3, 2):
                g_wait(p, step - 1, d)
            for d in (2, 1, 3):
                g_send(p, step, d).start()
    for p in range(3):
        h_copy(p, here[orders[p][2]], k).start()
    for d in (1, 3, 2):
        for p in range(3):
            g_wait(p, 2, d)
            h_copy(p, peer(orders[p][2], d)[0], k).start()

    def rows_sent():
        for p in range(3):
            for step in range(3):
                for d in (1, 2, 3):
                    g_send(p, step, d).wait_send()
            for there in range(4):
                h_copy(p, there, k).wait_send()

    sent.append(rows_sent)

    for cp in loads[N_SMALL + 4 : N_SMALL + 6]:
        cp.wait()
    accg[...] = jnp.zeros_like(accg)
    accu[...] = jnp.zeros_like(accu)
    accs[...] = jnp.zeros_like(accs)
    accl[...] = jnp.zeros_like(accl)

    def project(core):
        def one(zz):
            at = pl.multiple_of(zz * QUARTER + core * PART, PART)
            turned = xb[core, 1, :, zz]
            turned = jnp.stack([turned[i, j] for j in range(4) for i in range(4)])
            rows = [xb[core, 0, zz], turned, xb[core, 2, :, :, zz]]
            rows = jnp.concatenate([r.reshape(TOTAL, THIRD) for r in rows], axis=1).astype(F32)
            squares = rows * rows
            total = squares[:, 0:128]
            for i in range(1, PART // 128):
                total = total + squares[:, i * 128 : (i + 1) * 128]
            accs[...] = accs[...] + total
            rows = (rows * gainf[:, pl.ds(at, PART)]).astype(BF16)
            accg[...] = accg[...] + dot(rows, wgb[pl.ds(at, PART), :])
            accu[...] = accu[...] + dot(rows, wub[pl.ds(at, PART), :])
            accl[...] = accl[...] + dot_t(rows, rpad[:, pl.ds(at, PART)])

        each(EXP, one)

    project(k)
    for p in range(3):
        for there in range(4):
            h_copy(p, there, 1 - k).wait_recv()
    project(1 - k)
    scale = lax.rsqrt(jnp.sum(accs[...], axis=1, keepdims=True) / WIDTH + NORM_EPS)
    gate = accg[...] * scale
    logits = accl[...] * scale
    first, second = rcol[:, 0:1], rcol[:, 1:2]
    expert = iota((TOTAL, PAIR), 1).astype(F32)
    here_e = z.astype(F32)
    mine = jnp.sum(jnp.where(expert == here_e, logits, 0.0), axis=1, keepdims=True)
    theirs = jnp.sum(jnp.where(expert == first + second - here_e, logits, 0.0), axis=1, keepdims=True)
    share = 1.0 / (1.0 + jnp.exp(theirs - mine))
    share = jnp.where((first == here_e) | (second == here_e), share, 0.0)
    units = (gate / (1.0 + jnp.exp(-gate)) * (accu[...] * scale) * share).astype(BF16)

    usnd[...] = units
    u_copy = remote(usnd, urcv, us.at[0], ur.at[0], sib, z)
    u_copy.start()
    sent.append(lambda: u_copy.wait_send())

    for cp in loads[N_SMALL + 6 :]:
        cp.wait()
    for i in range(CHIPS // 2):
        low = dot_t(units[i * 32 : (i + 1) * 32], adnb[i * 128 : (i + 1) * 128, :])
        lsnd[2 * i : 2 * i + 2] = low.astype(BF16).reshape(2, PAIR, 128)

    def low_copy(i):
        chip = chip_at(i)
        return remote(lsnd.at[chip], lrcv.at[c], ls.at[i], lr.at[c], chip * 2 + k, z)

    for i in range(1, CHIPS):
        low_copy(i).start()
    sent.append(lambda: [low_copy(i).wait_send() for i in range(1, CHIPS)])
    lrcv[c] = lsnd[c]

    sum_orders = ("zyx", "xzy", "yxz")

    def part_of(t, step, there):
        if step == 1 and t == 2:
            return p3.at[t, :, there]
        return (p2, p3, p4)[step].at[t, there]

    def s_send(t, step, d):
        axis = sum_orders[t][step]
        there, seq, exp = peer(axis, d)
        return remote(
            part_of(t, step, there), (r2, r3, r4)[step].at[t, here[axis]],
            ss.at[t, step, d], sr.at[t, step, here[axis]], seq, exp,
        )

    def s_sum(t, step):
        axis = sum_orders[t][step]
        into = (r2, r3, r4)[step]
        total = part_of(t, step, here[axis])[...].astype(F32)
        for d in (1, 3, 2):
            there, seq, exp = peer(axis, d)
            remote(
                part_of(t, step, here[axis]), into.at[t, there],
                ss.at[t, step, 0], sr.at[t, step, there], seq, exp,
            ).wait_recv()
            total = total + into[t, there].astype(F32)
        return total

    def s_start(t, step):
        for d in (2, 1, 3):
            s_send(t, step, d).start()

    u_copy.wait_recv()
    for cp in down_copies:
        cp.wait_recv()
    both_units = jnp.concatenate([units, urcv[...]], axis=1)
    for t in range(3):
        for zz in range(EXP):
            at = zz * PART + t * THIRD
            both = dot(both_units, wdb[:, at : at + THIRD]).astype(BF16).reshape(4, 4, PAIR, THIRD)
            if t == 0:
                p2[t, zz] = both
            elif t == 1:
                for i in range(4):
                    p2[t, i, zz] = both[:, i]
            else:
                p2[t, :, zz] = both
        s_start(t, 0)
    sent.append(
        lambda: [s_send(t, i, d).wait_send() for t in range(3) for i in range(3) for d in (1, 2, 3)]
    )

    for i in range(1, CHIPS):
        chip = chip_at(i)
        remote(lsnd.at[chip], lrcv.at[chip], ls.at[0], lr.at[chip], chip * 2 + k, z).wait_recv()
    low = jnp.sum(lrcv[...].astype(F32), axis=0)
    lpair[0] = low.astype(BF16)
    lp_copy = remote(lpair.at[0], lpair.at[1], lps.at[0], lpr.at[0], sib, z)
    lp_copy.start()
    sent.append(lambda: lp_copy.wait_send())
    for cp in up_copies:
        cp.wait_recv()
    lp_copy.wait_recv()
    low = low + lpair[1].astype(F32)
    low = jnp.where(lax.div(lane16, 16) == lax.rem(ten_rows, 8), low, 0.0).astype(BF16)
    for zz in range(EXP):
        asnd[zz] = dot(low, upb[:, zz * PART : (zz + 1) * PART]).astype(BF16)

    def a_copy(d):
        zz = lax.rem(z + d, EXP)
        return remote(asnd.at[zz], arcv.at[z], as_.at[d], ar.at[z], s, zz)

    for d in (2, 1, 3):
        a_copy(d).start()
    sent.append(lambda: [a_copy(d).wait_send() for d in (1, 2, 3)])

    for t in range(3):
        p3[t] = s_sum(t, 0).astype(BF16)
        s_start(t, 1)
    for t in range(3):
        p4[t] = s_sum(t, 1).astype(BF16)
        s_start(t, 2)
    adapter = asnd[z].astype(F32)
    for d in (1, 3, 2):
        zz = lax.rem(z + d, EXP)
        remote(asnd.at[z], arcv.at[zz], as_.at[0], ar.at[zz], s, zz).wait_recv()
        adapter = adapter + arcv[zz].astype(F32)
    total = jnp.concatenate([s_sum(t, 2) for t in range(3)], axis=1) + adapter

    theirs = jnp.where(k == 0, total[ROWS:], total[:ROWS])
    fpair[0] = jnp.concatenate([theirs[:, : PART // 2], theirs[:, PART // 2 :]], axis=0).astype(BF16)
    f_copy = remote(fpair.at[0], fpair.at[1], fs.at[0], fr.at[0], sib, z)
    f_copy.start()
    sent.append(lambda: f_copy.wait_send())
    mine = jnp.where(k == 0, total[:ROWS], total[ROWS:])
    resid = [[xb[own_block(p, kk)].astype(F32) for p in range(3)] for kk in range(2)]
    resid = [jnp.concatenate(r, axis=1) for r in resid]
    resid = [jnp.where(k == 0, r[:ROWS], r[ROWS:]) for r in resid]
    f_copy.wait_recv()
    got = fpair[1].astype(F32)
    got = jnp.concatenate([got[:ROWS], got[ROWS:]], axis=1)
    got = [jnp.where(k == kk, mine, got) for kk in range(2)]
    out[...] = jnp.concatenate([r + g for r, g in zip(resid, got)], axis=1).astype(BF16)

    for wait in sent:
        wait()


def on_device(
    hidden, queries, suffix_row_keys, suffix_row_values, prefix_cached_keys, prefix_cached_values,
    expert_norm_gain, router, gate_weight, up_weight, down_weight, adapter_down_maps,
    adapter_up_maps, routes, tenants, lengths,
):
    vmem = pl.BlockSpec(memory_space=pltpu.VMEM)
    hbm = pl.BlockSpec(memory_space=pl.ANY)
    dma = pltpu.SemaphoreType.DMA
    scratch = [
        pltpu.SMEM((TOTAL,), jnp.int32),
        pltpu.SMEM((64,), jnp.int32),
        pltpu.VMEM((ROWS, QUARTER), BF16),
        pltpu.VMEM((ROWS, QUARTER), BF16),
        pltpu.VMEM((ROWS, KV * HEAD), BF16),
        pltpu.VMEM((ROWS, KV * HEAD), BF16),
        pltpu.VMEM((EXP, WIDTH), BF16),
        pltpu.VMEM((2, TOTAL), jnp.int32),
        pltpu.VMEM((WIDTH,), BF16),
        pltpu.VMEM((1, WIDTH), F32),
        pltpu.VMEM((MSG, HEAD), BF16),
        pltpu.VMEM((2, MSG, HEAD), BF16),
        pltpu.VMEM((CHIPS, BLK, HEAD), BF16),
        pltpu.VMEM((2 * PREFIX, HEAD), BF16),
        pltpu.VMEM((2 * PREFIX, HEAD), BF16),
        pltpu.VMEM((CHIPS, MSG, HEAD), BF16),
        pltpu.VMEM((CHIPS, MSG, HEAD), BF16),
        pltpu.VMEM((2, GROUP, ROWS, HEAD), F32),
        pltpu.VMEM((PAIR, 128), F32),
        pltpu.VMEM((PREFIX, HEAD), BF16),
        pltpu.VMEM((PREFIX, HEAD), BF16),
        pltpu.VMEM((2, 3, 4, 4, 4, PAIR, THIRD), BF16),
        pltpu.VMEM((WIDTH, UNITS), BF16),
        pltpu.VMEM((WIDTH, UNITS), BF16),
        pltpu.VMEM((2 * UNITS, HALF), BF16),
        pltpu.VMEM((1024, UNITS), BF16),
        pltpu.VMEM((128, HALF), BF16),
        pltpu.VMEM((TOTAL, UNITS), F32),
        pltpu.VMEM((TOTAL, UNITS), F32),
        pltpu.VMEM((TOTAL, 128), F32),
        pltpu.VMEM((TOTAL, PAIR), F32),
        pltpu.VMEM((PAIR, WIDTH), BF16),
        pltpu.VMEM((TOTAL, PAIR), F32),
        pltpu.VMEM((CHIPS, PAIR, 128), BF16),
        pltpu.VMEM((CHIPS, PAIR, 128), BF16),
        pltpu.VMEM((2, PAIR, 128), BF16),
        pltpu.VMEM((EXP, PAIR, PART), BF16),
        pltpu.VMEM((EXP, PAIR, PART), BF16),
        pltpu.VMEM((TOTAL, UNITS), BF16),
        pltpu.VMEM((TOTAL, UNITS), BF16),
        pltpu.VMEM((3, 4, 4, 4, PAIR, THIRD), BF16),
        pltpu.VMEM((3, 4, 4, 4, PAIR, THIRD), BF16),
        pltpu.VMEM((3, 4, 4, PAIR, THIRD), BF16),
        pltpu.VMEM((3, 4, 4, PAIR, THIRD), BF16),
        pltpu.VMEM((3, 4, PAIR, THIRD), BF16),
        pltpu.VMEM((3, 4, PAIR, THIRD), BF16),
        pltpu.VMEM((2, PAIR, PART // 2), BF16),
        dma((24,)),
        dma((1,)),
        dma((1,)),
        dma((2,)),
        dma((2,)),
        dma((CHIPS,)),
        dma((CHIPS,)),
        dma((CHIPS,)),
        dma((CHIPS,)),
        dma((3, 3, 4)),
        dma((3, 3, 4)),
        dma((3, 4)),
        dma((3, 4)),
        dma((4,)),
        dma((4,)),
        dma((CHIPS,)),
        dma((CHIPS,)),
        dma((1,)),
        dma((1,)),
        dma((4,)),
        dma((4,)),
        dma((4,)),
        dma((4,)),
        dma((1,)),
        dma((1,)),
        dma((3, 3, 4)),
        dma((3, 3, 4)),
        dma((1,)),
        dma((1,)),
    ]
    return pl.pallas_call(
        kernel,
        out_shape=jax.ShapeDtypeStruct((ROWS, QUARTER), BF16),
        in_specs=[hbm] * 16,
        out_specs=vmem,
        scratch_shapes=scratch,
        compiler_params=pltpu.CompilerParams(
            collective_id=0, has_side_effects=True, vmem_limit_bytes=58 * 1024 * 1024
        ),
        cost_estimate=pl.CostEstimate(flops=5 * 10**9, bytes_accessed=13 * 2**20, transcendentals=7 * 10**6),
        name="layer",
    )(
        hidden, queries, suffix_row_keys, suffix_row_values, prefix_cached_keys,
        prefix_cached_values, expert_norm_gain, router.T,
        gate_weight.reshape(WIDTH, UNITS), up_weight.reshape(WIDTH, UNITS),
        down_weight.reshape(UNITS, WIDTH), adapter_down_maps.reshape(-1, UNITS),
        adapter_up_maps.reshape(-1, WIDTH), routes.T, tenants, lengths,
    )


def solution(mesh):
    in_specs = (
        P("seq", "exp"),
        P("seq", "exp"),
        P("seq", "exp"),
        P("seq", "exp"),
        P("seq", "exp"),
        P("seq", "exp"),
        P(),
        P(),
        P("exp", None, "seq"),
        P("exp", None, "seq"),
        P("exp", "seq", None),
        P(None, "exp", None, "seq"),
        P("seq", "exp", None, None),
        P(),
        P(),
        P(),
    )
    return jax.shard_map(
        on_device, mesh=mesh, in_specs=in_specs, out_specs=P("seq", "exp"), check_vma=False
    )
```

time: 76.4 us -> 72.3 us (0.946)
  Pallas kernels: 74.8 us -> 70.8 us
    pallas_call x1, Pallas kernels: 74.8 us -> 70.8 us  [on_device(): pl.pallas_call(kernel, out_shape=jax.ShapeDtypeStruct((ROWS, QUARTER), BF...]
where the time goes in v3:
time: 72.3 us; the launch traced here: 72.1 us
  Pallas kernels  70.8 us (98%)
  local copies, waits for them, and re-layouts  1.35 us (2%)
    pallas_call x1, Pallas kernels, on_device(): pl.pallas_call(kernel, out_shape=jax.ShapeDtypeStruct((ROWS, QUARTER), BF...  70.8 us

profile of v3, /device:TPU:1, one launch (start us, length us, event | category | flops | bytes accessed | tf_op | source)
XLA Modules:
  0.0 72.1 jit_solution(10165314817920970200)
XLA Ops:
  0.0 70.8 %layer.1 = bf16[8,1536]{1,0:T(8,128)(2,1)} custom-call(bf16[8,1536]{1,0:T(8,128)(2,1)} %hid.1, bf16[8,1536]{1,0:T(8,128)(2,1)} %qry.1, bf16[8,256]{1,0:T(8,128)(2,1)} %skey.1, bf16[8,256]{1,0:T(8,128)(2,1)} %sval.1, bf16[2048,256]{1,0:T(8,128)(2,1)} %pk.1, bf16[2048,256]{1,0:T(8,128)(2,1)} %pv.1, bf16[6144]{0:T(1024)(128)(2,1)} %gain.1, ...), custom_call_target="tpu_custom_call" | custom-call | flops 5000000000 | bytes 13631488 | tf_op jit(solution)/shard_map/layer/pallas_call | solution.py:657
  70.8 1.3 %copy.18 = bf16[8,1536]{1,0:T(8,128)(2,1)} copy(bf16[8,1536]{1,0:T(8,128)(2,1)} %layer.1) | data formatting | bytes 49152

commit v4 on v3

--- a/solution.py
+++ b/solution.py
@@ -31,6 +31,7 @@
 MSG = BLK + 16
 PART = GROUP * HEAD
 THIRD = PART // 3
+AHEAD = (1, 3, 2, 0)
 KEYS = 512
 NORM_EPS = 1e-05
 LOG2E = 1.4426950408889634
@@ -72,7 +73,7 @@
     tenants, lengths,
     hid_v, qry_v, skey_v, sval_v, rout_v, routes_v, gain_v, gainf, msnd, pairb, qall, kbuf, vbuf, sbuf, pbuf,
     suf_o, suf_l, ksnd, vsnd, xb, wgb, wub, wdb, adnb, upb,
-    accg, accu, accs, accl, rpad, rcol, lsnd, lrcv, lpair, asnd, arcv, usnd, urcv,
+    accg, accu, accs, accl, rpad, rcol, lsnd, lrcv, lsum, lrow, lpair, asnd, arcv, usnd, urcv,
     p2, r2, p3, r3, p4, r4, fpair,
     lsem, ms, mr, ks, kr, qs, qr, ps, pr, gs, gr, hs, hr, ups, upr, ls, lr, lps, lpr, as_, ar,
     ds, dr, us, ur, ss, sr, fs, fr,
@@ -107,11 +108,11 @@
     def greet(seq, exp):
         pl.semaphore_signal(barrier, inc=1, device_id=(seq, exp), device_id_type=MESH)
 
+    for i in (10, 6, 14, 9, 11, 2, 8, 5, 7, 13, 15, 1, 3, 4, 12):
+        greet(chip_at(i) * 2 + k, z)
+    for d in (2, 1, 3):
+        greet(s, lax.rem(z + d, EXP))
     greet(sib, z)
-    for i in range(1, CHIPS):
-        greet(chip_at(i) * 2 + k, z)
-    for d in range(1, EXP):
-        greet(s, lax.rem(z + d, EXP))
 
     own_head = pl.ds(pl.multiple_of(k * HEAD, HEAD), HEAD)
     sib_head = pl.ds(pl.multiple_of(HEAD - k * HEAD, HEAD), HEAD)
@@ -176,15 +177,15 @@
 
     own = [pairb[kk, 0:QB, :] for kk in range(2)]
     qall[c] = jnp.concatenate(own, axis=0)
-    order = (1, 2, 3, 12, 13, 14, 15, 8, 9, 10, 11, 4, 5, 6, 7)
+    order = (12, 13, 14, 15, 4, 5, 6, 7, 8, 9, 10, 11, 1, 2, 3)
 
     def q_send(i):
         return remote(qall.at[c], qall.at[c], qs.at[i], qr.at[c], chip_at(i) * 2 + k, z)
 
-    for i in order[:3]:
+    for i in order[:4]:
         q_send(i).start()
     kv_copies[0].start()
-    for i in order[3:]:
+    for i in order[4:]:
         q_send(i).start()
     kv_copies[1].start()
     sent.append(lambda: [q_send(i).wait_send() for i in order])
@@ -267,10 +268,11 @@
 
     def scores(u, at):
         if at == 0:
-            for i in range(4 * u, 4 * u + 4):
+            a = AHEAD[u]
+            for i in range(4 * a, 4 * a + 4):
                 if i:
                     q_wait(i)
-            queries[u] = qall[pl.ds(lax.rem(y + u, 4) * 4, 4)].reshape(4 * BLK, HEAD)
+            queries[u] = qall[pl.ds(lax.rem(y + a, 4) * 4, 4)].reshape(4 * BLK, HEAD)
         return dot_t(queries[u], kbuf[at : at + KEYS, :])
 
     def finish(u, m, acc):
@@ -281,10 +283,11 @@
         stat = jnp.zeros((8, ROWS, 128), F32)
         for j in range(GROUP):
             stat = jnp.where(lane == j, lse[:, j], stat)
-        at = pl.ds(lax.rem(y + u, 4) * 4, 4)
+        a = AHEAD[u]
+        at = pl.ds(lax.rem(y + a, 4) * 4, 4)
         sbuf[at, 0:BLK, :] = o
         sbuf[at, BLK:, :] = three_parts(stat).reshape(4, PAIR, 128).astype(BF16)
-        for i in range(4 * u, 4 * u + 4):
+        for i in range(4 * a, 4 * a + 4):
             if i:
                 p_copy(i).start()
 
@@ -312,30 +315,46 @@
     sent.append(lambda: [p_copy(i).wait_send() for i in range(1, CHIPS)])
 
     pbuf[c] = sbuf[c]
-    for i in range(1, CHIPS):
+
+    def p_wait(i):
         chip = chip_at(i)
         remote(sbuf.at[chip], pbuf.at[chip], ps.at[0], pr.at[chip], chip * 2 + k, z).wait_recv()
-    lses = whole_of(pbuf[:, BLK:, :].astype(F32))
-    top = jnp.maximum(jnp.max(lses, axis=0), suf_l[...])
-    shares = jnp.exp2(lses - top[None])
-    suf_share = jnp.exp2(suf_l[...] - top)
-    inverse = 1.0 / (jnp.sum(shares, axis=0) + suf_share)
-    suf_share = suf_share * inverse
-    att = {}
+
+    def merged(rows, top, mass, att):
+        at = [pl.ds(lax.rem(y + a, 4) * 4, 4) for a in rows]
+        lses = whole_of(jnp.concatenate([pbuf[i, BLK:, :] for i in at], axis=0).astype(F32))
+        new = jnp.maximum(top, jnp.max(lses, axis=0))
+        shares = jnp.exp2(lses - new[None])
+        old = jnp.exp2(top - new)
+        mass = mass * old + jnp.sum(shares, axis=0)
+        for kk in range(2):
+            side = slice(kk * ROWS, (kk + 1) * ROWS)
+            for j in range(GROUP):
+                att[kk, j] = old[side, j : j + 1] * att[kk, j]
+        for n, i in enumerate(at):
+            part = pbuf[i, 0:BLK, :].astype(F32)
+            for m in range(4):
+                for kk in range(2):
+                    side = slice(kk * ROWS, (kk + 1) * ROWS)
+                    for j in range(GROUP):
+                        tile = part[m, (kk * GROUP + j) * ROWS : (kk * GROUP + j + 1) * ROWS]
+                        att[kk, j] = att[kk, j] + shares[4 * n + m, side, j : j + 1] * tile
+        return new, mass, att
+
+    att = {(kk, j): suf_o[kk, j] for kk in range(2) for j in range(GROUP)}
+    state = suf_l[...], jnp.ones((PAIR, 128), F32), att
+    for i in range(4, CHIPS):
+        p_wait(i)
+    state = merged((1, 2, 3), *state)
+    for i in range(1, 4):
+        p_wait(i)
+    _, mass, att = merged((0,), *state)
+    inverse = 1.0 / mass
     for kk in range(2):
-        rows = slice(kk * ROWS, (kk + 1) * ROWS)
+        side = slice(kk * ROWS, (kk + 1) * ROWS)
         hidden = pairb[kk, QB : 2 * QB, :].astype(F32)
         for j in range(GROUP):
-            own = suf_share[rows, j : j + 1] * suf_o[kk, j]
-            att[kk, j] = hidden[j * ROWS : (j + 1) * ROWS] + own
-    for i in range(CHIPS):
-        part = pbuf[i, 0:BLK, :].astype(F32)
-        share = shares[i] * inverse
-        for kk in range(2):
-            rows = slice(kk * ROWS, (kk + 1) * ROWS)
-            for j in range(GROUP):
-                at = (kk * GROUP + j) * ROWS
-                att[kk, j] = att[kk, j] + share[rows, j : j + 1] * part[at : at + ROWS]
+            att[kk, j] = hidden[j * ROWS : (j + 1) * ROWS] + inverse[side, j : j + 1] * att[kk, j]
 
     here = {"x": x, "y": y, "z": z}
     orders = ("xyz", "yzx", "zxy")
@@ -449,16 +468,31 @@
         cp.wait()
     for i in range(CHIPS // 2):
         low = dot_t(units[i * 32 : (i + 1) * 32], adnb[i * 128 : (i + 1) * 128, :])
-        lsnd[2 * i : 2 * i + 2] = low.astype(BF16).reshape(2, PAIR, 128)
-
-    def low_copy(i):
-        chip = chip_at(i)
-        return remote(lsnd.at[chip], lrcv.at[c], ls.at[i], lr.at[c], chip * 2 + k, z)
-
-    for i in range(1, CHIPS):
-        low_copy(i).start()
-    sent.append(lambda: [low_copy(i).wait_send() for i in range(1, CHIPS)])
-    lrcv[c] = lsnd[c]
+        for j in range(2):
+            lsnd[i % 2 * 2 + j, i // 2] = low[j * PAIR : (j + 1) * PAIR].astype(BF16)
+
+    def low_copy(step, d):
+        axis = "xy"[step]
+        there, seq, exp = peer(axis, d)
+        src, dst = ((lsnd, lrcv), (lsum, lrow))[step]
+        mine = here[axis]
+        return remote(src.at[there], dst.at[mine], ls.at[step, d], lr.at[step, mine], seq, exp)
+
+    def low_sum(step):
+        axis = "xy"[step]
+        src, dst = ((lsnd, lrcv), (lsum, lrow))[step]
+        total = src[here[axis]].astype(F32)
+        for d in (1, 3, 2):
+            there, seq, exp = peer(axis, d)
+            remote(
+                src.at[here[axis]], dst.at[there], ls.at[step, 0], lr.at[step, there], seq, exp
+            ).wait_recv()
+            total = total + dst[there].astype(F32)
+        return total
+
+    for d in (2, 1, 3):
+        low_copy(0, d).start()
+    sent.append(lambda: [low_copy(step, d).wait_send() for step in range(2) for d in (1, 2, 3)])
 
     sum_orders = ("zyx", "xzy", "yxz")
 
@@ -512,10 +546,14 @@
         lambda: [s_send(t, i, d).wait_send() for t in range(3) for i in range(3) for d in (1, 2, 3)]
     )
 
-    for i in range(1, CHIPS):
-        chip = chip_at(i)
-        remote(lsnd.at[chip], lrcv.at[chip], ls.at[0], lr.at[chip], chip * 2 + k, z).wait_recv()
-    low = jnp.sum(lrcv[...].astype(F32), axis=0)
+    lsum[...] = low_sum(0).astype(BF16)
+    for d in (2, 1, 3):
+        low_copy(1, d).start()
+    for t in range(3):
+        p3[t] = s_sum(t, 0).astype(BF16)
+        s_start(t, 1)
+
+    low = low_sum(1)
     lpair[0] = low.astype(BF16)
     lp_copy = remote(lpair.at[0], lpair.at[1], lps.at[0], lpr.at[0], sib, z)
     lp_copy.start()
@@ -536,9 +574,6 @@
         a_copy(d).start()
     sent.append(lambda: [a_copy(d).wait_send() for d in (1, 2, 3)])
 
-    for t in range(3):
-        p3[t] = s_sum(t, 0).astype(BF16)
-        s_start(t, 1)
     for t in range(3):
         p4[t] = s_sum(t, 1).astype(BF16)
         s_start(t, 2)
@@ -610,8 +645,10 @@
         pltpu.VMEM((TOTAL, PAIR), F32),
         pltpu.VMEM((PAIR, WIDTH), BF16),
         pltpu.VMEM((TOTAL, PAIR), F32),
-        pltpu.VMEM((CHIPS, PAIR, 128), BF16),
-        pltpu.VMEM((CHIPS, PAIR, 128), BF16),
+        pltpu.VMEM((4, 4, PAIR, 128), BF16),
+        pltpu.VMEM((4, 4, PAIR, 128), BF16),
+        pltpu.VMEM((4, PAIR, 128), BF16),
+        pltpu.VMEM((4, PAIR, 128), BF16),
         pltpu.VMEM((2, PAIR, 128), BF16),
         pltpu.VMEM((EXP, PAIR, PART), BF16),
         pltpu.VMEM((EXP, PAIR, PART), BF16),
@@ -639,8 +676,8 @@
         dma((3, 4)),
         dma((4,)),
         dma((4,)),
-        dma((CHIPS,)),
-        dma((CHIPS,)),
+        dma((2, 4)),
+        dma((2, 4)),
         dma((1,)),
         dma((1,)),
         dma((4,)),

time: 72.3 us -> 70.8 us (0.979)
  Pallas kernels: 70.8 us -> 69.3 us
    pallas_call x1, Pallas kernels: 70.8 us -> 69.3 us  [on_device(): pl.pallas_call(kernel, out_shape=jax.ShapeDtypeStruct((ROWS, QUARTER), BF...]
where the time goes in v4:
time: 70.8 us; the launch traced here: 70.6 us
  Pallas kernels  69.3 us (98%)
  local copies, waits for them, and re-layouts  1.35 us (2%)
    pallas_call x1, Pallas kernels, on_device(): pl.pallas_call(kernel, out_shape=jax.ShapeDtypeStruct((ROWS, QUARTER), BF...  69.3 us

profile of v4, /device:TPU:1, one launch (start us, length us, event | category | flops | bytes accessed | tf_op | source)
XLA Modules:
  0.0 70.6 jit_solution(14495537742691881678)
XLA Ops:
  0.0 69.3 %layer.1 = bf16[8,1536]{1,0:T(8,128)(2,1)} custom-call(bf16[8,1536]{1,0:T(8,128)(2,1)} %hid.1, bf16[8,1536]{1,0:T(8,128)(2,1)} %qry.1, bf16[8,256]{1,0:T(8,128)(2,1)} %skey.1, bf16[8,256]{1,0:T(8,128)(2,1)} %sval.1, bf16[2048,256]{1,0:T(8,128)(2,1)} %pk.1, bf16[2048,256]{1,0:T(8,128)(2,1)} %pv.1, bf16[6144]{0:T(1024)(128)(2,1)} %gain.1, ...), custom_call_target="tpu_custom_call" | custom-call | flops 5000000000 | bytes 13631488 | tf_op jit(solution)/shard_map/layer/pallas_call | solution.py:694
  69.3 1.3 %copy.18 = bf16[8,1536]{1,0:T(8,128)(2,1)} copy(bf16[8,1536]{1,0:T(8,128)(2,1)} %layer.1) | data formatting | bytes 49152

commit v5 on v4

--- a/solution.py
+++ b/solution.py
@@ -418,13 +418,9 @@
 
     for cp in loads[N_SMALL + 4 : N_SMALL + 6]:
         cp.wait()
-    accg[...] = jnp.zeros_like(accg)
-    accu[...] = jnp.zeros_like(accu)
-    accs[...] = jnp.zeros_like(accs)
-    accl[...] = jnp.zeros_like(accl)
-
-    def project(core):
-        def one(zz):
+
+    def project(core, sums):
+        for zz in range(EXP):
             at = pl.multiple_of(zz * QUARTER + core * PART, PART)
             turned = xb[core, 1, :, zz]
             turned = jnp.stack([turned[i, j] for j in range(4) for i in range(4)])
@@ -434,22 +430,25 @@
             total = squares[:, 0:128]
             for i in range(1, PART // 128):
                 total = total + squares[:, i * 128 : (i + 1) * 128]
-            accs[...] = accs[...] + total
             rows = (rows * gainf[:, pl.ds(at, PART)]).astype(BF16)
-            accg[...] = accg[...] + dot(rows, wgb[pl.ds(at, PART), :])
-            accu[...] = accu[...] + dot(rows, wub[pl.ds(at, PART), :])
-            accl[...] = accl[...] + dot_t(rows, rpad[:, pl.ds(at, PART)])
-
-        each(EXP, one)
-
-    project(k)
+            got = (
+                total,
+                dot(rows, wgb[pl.ds(at, PART), :]),
+                dot(rows, wub[pl.ds(at, PART), :]),
+                dot_t(rows, rpad[:, pl.ds(at, PART)]),
+            )
+            sums = got if sums is None else tuple(a + b for a, b in zip(sums, got))
+        return sums
+
+    for ref, value in zip((accs, accg, accu, accl), project(k, None)):
+        ref[...] = value
     for p in range(3):
         for there in range(4):
             h_copy(p, there, 1 - k).wait_recv()
-    project(1 - k)
-    scale = lax.rsqrt(jnp.sum(accs[...], axis=1, keepdims=True) / WIDTH + NORM_EPS)
-    gate = accg[...] * scale
-    logits = accl[...] * scale
+    squares, gate, up, logits = project(1 - k, tuple(ref[...] for ref in (accs, accg, accu, accl)))
+    scale = lax.rsqrt(jnp.sum(squares, axis=1, keepdims=True) / WIDTH + NORM_EPS)
+    gate = gate * scale
+    logits = logits * scale
     first, second = rcol[:, 0:1], rcol[:, 1:2]
     expert = iota((TOTAL, PAIR), 1).astype(F32)
     here_e = z.astype(F32)
@@ -457,7 +456,7 @@
     theirs = jnp.sum(jnp.where(expert == first + second - here_e, logits, 0.0), axis=1, keepdims=True)
     share = 1.0 / (1.0 + jnp.exp(theirs - mine))
     share = jnp.where((first == here_e) | (second == here_e), share, 0.0)
-    units = (gate / (1.0 + jnp.exp(-gate)) * (accu[...] * scale) * share).astype(BF16)
+    units = (gate / (1.0 + jnp.exp(-gate)) * (up * scale) * share).astype(BF16)
 
     usnd[...] = units
     u_copy = remote(usnd, urcv, us.at[0], ur.at[0], sib, z)

time: 70.8 us -> 70.1 us (level)
  no operation moved by 1% of the time
where the time goes in v5:
time: 70.1 us; the launch traced here: 70 us
  Pallas kernels  68.6 us (98%)
  local copies, waits for them, and re-layouts  1.35 us (2%)
    pallas_call x1, Pallas kernels, on_device(): pl.pallas_call(kernel, out_shape=jax.ShapeDtypeStruct((ROWS, QUARTER), BF...  68.6 us

profile of v5, /device:TPU:1, one launch (start us, length us, event | category | flops | bytes accessed | tf_op | source)
XLA Modules:
  0.0 70.0 jit_solution(15746242609775229710)
XLA Ops:
  0.0 68.6 %layer.1 = bf16[8,1536]{1,0:T(8,128)(2,1)} custom-call(bf16[8,1536]{1,0:T(8,128)(2,1)} %hid.1, bf16[8,1536]{1,0:T(8,128)(2,1)} %qry.1, bf16[8,256]{1,0:T(8,128)(2,1)} %skey.1, bf16[8,256]{1,0:T(8,128)(2,1)} %sval.1, bf16[2048,256]{1,0:T(8,128)(2,1)} %pk.1, bf16[2048,256]{1,0:T(8,128)(2,1)} %pv.1, bf16[6144]{0:T(1024)(128)(2,1)} %gain.1, ...), custom_call_target="tpu_custom_call" | custom-call | flops 5000000000 | bytes 13631488 | tf_op jit(solution)/shard_map/layer/pallas_call | solution.py:693
  68.6 1.3 %copy.18 = bf16[8,1536]{1,0:T(8,128)(2,1)} copy(bf16[8,1536]{1,0:T(8,128)(2,1)} %layer.1) | data formatting | bytes 49152

commit v6 on v5

--- a/solution.py
+++ b/solution.py
@@ -525,6 +525,7 @@
         for d in (2, 1, 3):
             s_send(t, step, d).start()
 
+    ahead = [dot(units, wdb[0:UNITS, zz * PART : zz * PART + THIRD]) for zz in range(EXP)]
     u_copy.wait_recv()
     for cp in down_copies:
         cp.wait_recv()
@@ -532,7 +533,11 @@
     for t in range(3):
         for zz in range(EXP):
             at = zz * PART + t * THIRD
-            both = dot(both_units, wdb[:, at : at + THIRD]).astype(BF16).reshape(4, 4, PAIR, THIRD)
+            if t == 0:
+                both = ahead[zz] + dot(urcv[...], wdb[UNITS:, at : at + THIRD])
+            else:
+                both = dot(both_units, wdb[:, at : at + THIRD])
+            both = both.astype(BF16).reshape(4, 4, PAIR, THIRD)
             if t == 0:
                 p2[t, zz] = both
             elif t == 1:

time: 70.1 us -> 70.1 us (level)
  no operation moved by 1% of the time
where the time goes in v6:
time: 70.1 us; the launch traced here: 70 us
  Pallas kernels  68.6 us (98%)
  local copies, waits for them, and re-layouts  1.35 us (2%)
    pallas_call x1, Pallas kernels, on_device(): pl.pallas_call(kernel, out_shape=jax.ShapeDtypeStruct((ROWS, QUARTER), BF...  68.6 us

profile of v6, /device:TPU:1, one launch (start us, length us, event | category | flops | bytes accessed | tf_op | source)
XLA Modules:
  0.0 70.0 jit_solution(3757846385134179646)
XLA Ops:
  0.0 68.6 %layer.1 = bf16[8,1536]{1,0:T(8,128)(2,1)} custom-call(bf16[8,1536]{1,0:T(8,128)(2,1)} %hid.1, bf16[8,1536]{1,0:T(8,128)(2,1)} %qry.1, bf16[8,256]{1,0:T(8,128)(2,1)} %skey.1, bf16[8,256]{1,0:T(8,128)(2,1)} %sval.1, bf16[2048,256]{1,0:T(8,128)(2,1)} %pk.1, bf16[2048,256]{1,0:T(8,128)(2,1)} %pv.1, bf16[6144]{0:T(1024)(128)(2,1)} %gain.1, ...), custom_call_target="tpu_custom_call" | custom-call | flops 5000000000 | bytes 13631488 | tf_op jit(solution)/shard_map/layer/pallas_call | solution.py:698
  68.6 1.3 %copy.18 = bf16[8,1536]{1,0:T(8,128)(2,1)} copy(bf16[8,1536]{1,0:T(8,128)(2,1)} %layer.1) | data formatting | bytes 49152
